TPU v7x, 128 devices: a whole 4x4x4 slice. The times are simulated.
128 devices in a mesh: dp: 32 (over y, x, core), tensor: 4 (over z).
Axes of the slice: x: 4, y: 4, z: 4, core: 2. Of those that a mesh axis runs over, the one named last changes fastest.
Arguments:
- tokens: bfloat16 [16384, 2048], P(('dp', 'tensor')), may hold values from -6 to 6
- gain_attn: float32 [2048], replicated, may hold values from 0.5 to 1.5
- w_qkv: bfloat16 [3, 2048, 2048], P(None, None, 'tensor'), may hold values from -0.1875 to 0.1875
- w_out: bfloat16 [2048, 2048], P('tensor'), may hold values from -0.375 to 0.375
- gain_mlp: float32 [2048], replicated, may hold values from 0.5 to 1.5
- w_gate_up: bfloat16 [2, 2048, 5632], P(None, None, 'tensor'), may hold values from -0.125 to 0.125
- w_down: bfloat16 [5632, 2048], P('tensor'), may hold values from -0.15625 to 0.15625
- cotangent: bfloat16 [16384, 2048], P(('dp', 'tensor')), may hold values from -24 to 24
- lengths: int32 [32], P('dp'), may hold values from 385 to 512, as said below
Outputs:
- output: float32 [16384, 2048], P(('dp', 'tensor'))
- grad_tokens: float32 [16384, 2048], P(('dp', 'tensor'))
- grad_gain_attn: float32 [2048], replicated
- grad_qkv: float32 [3, 2048, 2048], P(None, 'dp', 'tensor')
- grad_out_proj: float32 [2048, 2048], P('tensor', 'dp')
- grad_gain_mlp: float32 [2048], replicated
- grad_gate_up: float32 [2, 2048, 5632], P(None, 'dp', 'tensor')
- grad_down: float32 [5632, 2048], P('tensor', 'dp')
Inputs may be any that keep to these rules, and one draw needn't show every extreme that they name: A sequence's live tokens are its first lengths[s] positions; the rest of its 512 rows are padding. Some sequence is full in every draw.
All inputs are finite; a program needn't handle non-finite values.
Results may differ from a plain program's by a relative error of at most 0.025.
Values may be sent and summed in bfloat16 or wider, within the bound.
A program may use at most 192 MiB of HBM per device.

v0:
```python
import math

import jax
import jax.numpy as jnp
from jax import lax
from jax.sharding import PartitionSpec as P

HD = 128


epsilon = 1e-05


def rotary_tables(length_rows, head_size):
    half_size = head_size // 2
    positions = jnp.arange(length_rows, dtype=jnp.float32)[:, None, None]
    frequency = jnp.exp(
        jnp.arange(half_size, dtype=jnp.float32) * (-2.0 * math.log(10000.0) / head_size)
    )
    angles = positions * frequency
    return (jnp.cos(angles), jnp.sin(angles))


def rotate(values_in, cos_table, sin_table):
    half_size = values_in.shape[-1] // 2
    first_half = values_in[..., :half_size]
    second_half = values_in[..., half_size:]
    return jnp.concatenate(
        [
            first_half * cos_table - second_half * sin_table,
            second_half * cos_table + first_half * sin_table,
        ],
        axis=-1,
    )


def unrotate(grads_in, cos_table, sin_table):
    half_size = grads_in.shape[-1] // 2
    first_half = grads_in[..., :half_size]
    second_half = grads_in[..., half_size:]
    return jnp.concatenate(
        [
            first_half * cos_table + second_half * sin_table,
            second_half * cos_table - first_half * sin_table,
        ],
        axis=-1,
    )


def allowed_mask(first_row, block_rows, length_rows, live_rows):
    query_rows = first_row + jnp.arange(block_rows, dtype=jnp.int32)[:, None]
    key_rows = jnp.arange(length_rows, dtype=jnp.int32)[None, :]
    return (key_rows <= query_rows) & (key_rows < live_rows)


def attend(queries, keys_rot, values_in, live_rows):
    length_rows, head_count, head_size = queries.shape
    block_rows = min(512, length_rows)
    blocks = length_rows // block_rows

    def one_block(block_item):
        query_block, block_index = block_item
        scores = jnp.einsum(
            "qhd,khd->hqk", query_block, keys_rot, preferred_element_type=jnp.float32
        )
        allowed = allowed_mask(block_index * block_rows, block_rows, length_rows, live_rows)
        scores = jnp.where(allowed[None], scores, -1e30)
        row_top = jnp.max(scores, axis=-1, keepdims=True)
        exps = jnp.exp(scores - row_top)
        row_total = jnp.sum(exps, axis=-1, keepdims=True)
        probs = (exps / row_total).astype(jnp.bfloat16)
        attended = jnp.einsum("hqk,khd->qhd", probs, values_in, preferred_element_type=jnp.float32)
        return (attended, (row_top + jnp.log(row_total))[..., 0])

    pieces, log_sums = lax.map(
        one_block,
        (
            queries.reshape(blocks, block_rows, head_count, head_size),
            jnp.arange(blocks, dtype=jnp.int32),
        ),
    )
    return (pieces.reshape(length_rows, head_count, head_size), log_sums)


def attend_back(queries, keys_rot, values_in, grad_context, log_sums, live_rows):
    length_rows, head_count, head_size = queries.shape
    block_rows = min(512, length_rows)
    blocks = length_rows // block_rows

    def one_block(running, block_item):
        grad_keys, grad_values = running
        query_block, grad_block, sums_block, block_index = block_item
        scores = jnp.einsum(
            "qhd,khd->hqk", query_block, keys_rot, preferred_element_type=jnp.float32
        )
        allowed = allowed_mask(block_index * block_rows, block_rows, length_rows, live_rows)
        scores = jnp.where(allowed[None], scores, -1e30)
        probs = jnp.exp(scores - sums_block[..., None])
        grad_probs = jnp.einsum(
            "qhd,khd->hqk", grad_block, values_in, preferred_element_type=jnp.float32
        )
        grad_values = grad_values + jnp.einsum(
            "hqk,qhd->khd",
            probs.astype(jnp.bfloat16),
            grad_block,
            preferred_element_type=jnp.float32,
        )
        inner = jnp.sum(probs * grad_probs, axis=-1, keepdims=True)
        grad_scores = (probs * (grad_probs - inner)).astype(jnp.bfloat16)
        grad_query = jnp.einsum(
            "hqk,khd->qhd", grad_scores, keys_rot, preferred_element_type=jnp.float32
        )
        grad_keys = grad_keys + jnp.einsum(
            "hqk,qhd->khd", grad_scores, query_block, preferred_element_type=jnp.float32
        )
        return ((grad_keys, grad_values), grad_query)

    empty_grads = jnp.zeros((length_rows, head_count, head_size), jnp.float32)
    block_shape = (blocks, block_rows, head_count, head_size)
    (grad_keys, grad_values), grad_queries = lax.scan(
        one_block,
        (empty_grads, empty_grads),
        (
            queries.reshape(block_shape),
            grad_context.reshape(block_shape),
            log_sums,
            jnp.arange(blocks, dtype=jnp.int32),
        ),
    )
    return (grad_queries.reshape(length_rows, head_count, head_size), grad_keys, grad_values)


def body(tokens, gain_attn, w_qkv, w_out, gain_mlp, w_gate_up, w_down, cotangent, lengths):
    local_rows = tokens.shape[0]
    head_count = w_qkv.shape[2] // HD
    live_rows = lengths[0]
    stream = tokens.astype(jnp.float32)
    inv_attn = lax.rsqrt(jnp.mean(stream * stream, axis=-1, keepdims=True) + epsilon)
    normed_attn = (stream * inv_attn * gain_attn).astype(jnp.bfloat16)
    whole_attn = lax.all_gather(normed_attn, "tensor", axis=0, tiled=True)
    length_rows = whole_attn.shape[0]
    projected = jnp.einsum("td,jdf->jtf", whole_attn, w_qkv, preferred_element_type=jnp.float32)
    cos_table, sin_table = rotary_tables(length_rows, HD)
    shape_heads = (length_rows, head_count, HD)
    queries = (
        rotate(projected[0].reshape(shape_heads), cos_table, sin_table) * HD ** (-0.5)
    ).astype(jnp.bfloat16)
    keys_rot = rotate(projected[1].reshape(shape_heads), cos_table, sin_table).astype(jnp.bfloat16)
    values_in = projected[2].reshape(shape_heads).astype(jnp.bfloat16)
    attended, log_sums = attend(queries, keys_rot, values_in, live_rows)
    context = attended.reshape(length_rows, head_count * HD).astype(jnp.bfloat16)
    middle = stream + lax.psum_scatter(
        jnp.dot(context, w_out, preferred_element_type=jnp.float32).astype(jnp.bfloat16),
        "tensor",
        scatter_dimension=0,
        tiled=True,
    ).astype(jnp.float32)
    inv_mlp = lax.rsqrt(jnp.mean(middle * middle, axis=-1, keepdims=True) + epsilon)
    normed_mlp = (middle * inv_mlp * gain_mlp).astype(jnp.bfloat16)
    whole_mlp = lax.all_gather(normed_mlp, "tensor", axis=0, tiled=True)
    gate_up = jnp.einsum("td,jdf->jtf", whole_mlp, w_gate_up, preferred_element_type=jnp.float32)
    gate_part = gate_up[0]
    up_part = gate_up[1]
    sigmoid_gate = jax.nn.sigmoid(gate_part)
    silu_gate = gate_part * sigmoid_gate
    hidden = (silu_gate * up_part).astype(jnp.bfloat16)
    output = middle + lax.psum_scatter(
        jnp.dot(hidden, w_down, preferred_element_type=jnp.float32).astype(jnp.bfloat16),
        "tensor",
        scatter_dimension=0,
        tiled=True,
    ).astype(jnp.float32)
    own_rows = lax.axis_index("tensor") * local_rows + jnp.arange(local_rows, dtype=jnp.int32)
    masked = cotangent * (own_rows < live_rows).astype(jnp.bfloat16)[:, None]
    whole_grad = lax.all_gather(masked, "tensor", axis=0, tiled=True)
    grad_hidden = jnp.einsum("td,fd->tf", whole_grad, w_down, preferred_element_type=jnp.float32)
    grad_down = jnp.einsum("tf,td->fd", hidden, whole_grad, preferred_element_type=jnp.float32)
    grad_gate = grad_hidden * up_part * sigmoid_gate * (1.0 + gate_part * (1.0 - sigmoid_gate))
    grad_up = grad_hidden * silu_gate
    grad_gate_up = jnp.stack([grad_gate, grad_up]).astype(jnp.bfloat16)
    portion = grad_gate_up
    grad_normed_mlp = lax.psum_scatter(
        jnp.einsum("jtf,jdf->td", portion, w_gate_up, preferred_element_type=jnp.float32).astype(
            jnp.bfloat16
        ),
        "tensor",
        scatter_dimension=0,
        tiled=True,
    ).astype(jnp.float32)
    grad_w_gate_up = jnp.einsum(
        "td,jtf->jdf", whole_mlp, grad_gate_up, preferred_element_type=jnp.float32
    )
    scaled_mlp = grad_normed_mlp * gain_mlp
    gain_mlp_part = jnp.sum(grad_normed_mlp * middle * inv_mlp, axis=0)
    grad_middle = (
        masked.astype(jnp.float32)
        + inv_mlp * scaled_mlp
        - middle * inv_mlp**3 * jnp.mean(middle * scaled_mlp, axis=-1, keepdims=True)
    )
    grad_branch = grad_middle.astype(jnp.bfloat16)
    whole_branch = lax.all_gather(grad_branch, "tensor", axis=0, tiled=True)
    grad_w_out = jnp.einsum("tf,td->fd", context, whole_branch, preferred_element_type=jnp.float32)
    grad_context = (
        jnp.einsum("td,fd->tf", whole_branch, w_out, preferred_element_type=jnp.float32)
        .astype(jnp.bfloat16)
        .reshape(shape_heads)
    )
    grad_queries, grad_keys, grad_values = attend_back(
        queries, keys_rot, values_in, grad_context, log_sums, live_rows
    )
    grad_projected = (
        jnp.stack(
            [
                unrotate(grad_queries, cos_table, sin_table) * HD ** (-0.5),
                unrotate(grad_keys, cos_table, sin_table),
                grad_values,
            ]
        )
        .reshape(3, length_rows, head_count * HD)
        .astype(jnp.bfloat16)
    )
    portion = grad_projected
    grad_normed_attn = lax.psum_scatter(
        jnp.einsum("jtf,jdf->td", portion, w_qkv, preferred_element_type=jnp.float32).astype(
            jnp.bfloat16
        ),
        "tensor",
        scatter_dimension=0,
        tiled=True,
    ).astype(jnp.float32)
    grad_w_qkv = jnp.einsum(
        "td,jtf->jdf", whole_attn, grad_projected, preferred_element_type=jnp.float32
    )
    scaled_attn = grad_normed_attn * gain_attn
    gain_attn_part = jnp.sum(grad_normed_attn * stream * inv_attn, axis=0)
    grad_tokens = (
        grad_middle
        + inv_attn * scaled_attn
        - stream * inv_attn**3 * jnp.mean(stream * scaled_attn, axis=-1, keepdims=True)
    )
    gain_grads = lax.psum((gain_attn_part, gain_mlp_part), ("dp", "tensor"))
    shares = (
        lax.psum_scatter(
            grad_w_qkv.astype(jnp.bfloat16), "dp", scatter_dimension=1, tiled=True
        ).astype(jnp.float32),
        lax.psum_scatter(
            grad_w_out.astype(jnp.bfloat16), "dp", scatter_dimension=1, tiled=True
        ).astype(jnp.float32),
        lax.psum_scatter(
            grad_w_gate_up.astype(jnp.bfloat16), "dp", scatter_dimension=1, tiled=True
        ).astype(jnp.float32),
        lax.psum_scatter(
            grad_down.astype(jnp.bfloat16), "dp", scatter_dimension=1, tiled=True
        ).astype(jnp.float32),
    )
    return (
        output,
        grad_tokens,
        gain_grads[0],
        shares[0],
        shares[1],
        gain_grads[1],
        shares[2],
        shares[3],
    )


def solution(mesh):
    placed = (
        P(("dp", "tensor"), None),
        P(),
        P(None, None, "tensor"),
        P("tensor", None),
        P(),
        P(None, None, "tensor"),
        P("tensor", None),
        P(("dp", "tensor"), None),
        P("dp"),
    )
    return jax.shard_map(
        body,
        mesh=mesh,
        in_specs=placed,
        out_specs=(
            P(("dp", "tensor"), None),
            P(("dp", "tensor"), None),
            P(),
            P(None, "dp", "tensor"),
            P("tensor", "dp"),
            P(),
            P(None, "dp", "tensor"),
            P("tensor", "dp"),
        ),
        check_vma=False,
    )
```

profile of v0, /device:TPU:1, one launch (start us, length us, event | category | flops | bytes accessed | tf_op | source)
XLA Modules:
  0.0 693.5 jit_solution(7852899398692805825)
XLA Ops:
  7.2 1.4 fusion.33
  8.6 2.0 fusion.35
  11.5 1.0 fusion.44
  12.5 32.6 %all-gather.5.cloned.1.call-done = bf16[512,2048]{1,0:T(8,128)(2,1)} async-done(((bf16[128,2048]{1,0:T(8,128)(2,1)}), bf16[512,2048]{1,0:T(8,128)(2,1)}) %all-gather.5.cloned.1.call-update) | async-done | bytes 2097168 | tf_op jit(solution)/shard_map/all_gather | solution.py:140
  45.1 6.3 fusion.14
  51.6 1.1 fusion.57
  52.7 1.1 fusion.56
  53.8 2.4 copy.103
  56.2 2.4 copy.101
  58.6 2.4 copy.102
  60.9 2.3 copy.100
  63.2 2.7 subtract_convert_fusion.1
  66.4 1.0 select_reduce_fusion
  67.4 0.8 fusion
  68.2 1.4 fusion.22
  69.6 0.8 copy-done.24
  70.4 2.6 convolution_convert_fusion.2
  73.1 29.9 %reduce-scatter.7.cloned.1.call-done = bf16[128,2048]{1,0:T(8,128)(2,1)} async-done(((bf16[512,2048]{1,0:T(8,128)(2,1)}), bf16[128,2048]{1,0:T(8,128)(2,1)}) %reduce-scatter.7.cloned.1.call-update) | async-done | bytes 524304 | tf_op jit(solution)/shard_map/reduce_scatter | solution.py:152
  103.0 1.3 multiply_reduce_fusion.1
  104.3 2.0 multiply_convert_fusion.4
  106.5 0.9 broadcast_multiply_fusion
  107.6 29.5 %all-gather.7.cloned.1.call-done = bf16[512,2048]{1,0:T(8,128)(2,1)} async-done(((bf16[128,2048]{1,0:T(8,128)(2,1)}), bf16[512,2048]{1,0:T(8,128)(2,1)}) %all-gather.7.cloned.1.call-update) | async-done | bytes 2097168 | tf_op jit(solution)/shard_map/all_gather | solution.py:160
  137.1 12.6 %convolution_bitcast_fusion = f32[2,512,1408]{2,1,0:T(8,128)} fusion(bf16[2,2048,1408]{2,1,0:T(8,128)(2,1)} %param.14, bf16[512,2048]{1,0:T(8,128)(2,1)} %all-gather.7.cloned.1.call-done), kind=kOutput, calls=%fused_computation.3 | convolution fusion | flops 5905580032 | bytes 19398656 | tf_op jit(solution)/shard_map/td,jdf->jtf/dot_general | solution.py:161
  149.7 20.6 %all-gather.9.cloned.1.call-done = bf16[512,2048]{1,0:T(8,128)(2,1)} async-done(((bf16[128,2048]{1,0:T(8,128)(2,1)}), bf16[512,2048]{1,0:T(8,128)(2,1)}) %all-gather.9.cloned.1.call-update) | async-done | bytes 2097168 | tf_op jit(solution)/shard_map/all_gather | solution.py:175
  170.3 10.4 %fusion.18 = (bf16[1,512,1408]{2,1,0:T(8,128)(2,1)S(1)}, bf16[1,512,1408]{2,1,0:T(8,128)(2,1)S(1)}, bf16[512,1408]{1,0:T(8,128)(2,1)}) fusion(f32[2,512,1408]{2,1,0:T(8,128)} %convolution_bitcast_fusion, bf16[512,2048]{1,0:T(8,128)(2,1)} %all-gather.9.cloned.1.call-done, bf16[1408,2048]{1,0:T(8,128)(2,1)} %param.15), kind=kOutput, calls=%fused_computation.44 | convolution fusion | flops 2963603456 | bytes 17956864 | tf_op jit(solution)/shard_map/td,fd->tf/dot_general | solution.py:176
  180.7 1.1 copy-done.26
  182.3 10.1 %bitcast_convert_fusion.1 = bf16[512,2048]{1,0:T(8,128)(2,1)} fusion(bf16[2,2048,1408]{2,1,0:T(8,128)(2,1)} %param.14, bf16[1,512,1408]{2,1,0:T(8,128)(2,1)S(1)} %get-tuple-element.92, bf16[1,512,1408]{2,1,0:T(8,128)(2,1)S(1)} %get-tuple-element.91), kind=kOutput, calls=%fused_computation.5 | convolution fusion | flops 5908070400 | bytes 16515072 | tf_op jit(solution)/shard_map/jtf,jdf->td/dot_general | solution.py:183
  192.4 29.9 %reduce-scatter.11.cloned.1.call-done = bf16[128,2048]{1,0:T(8,128)(2,1)} async-done(((bf16[512,2048]{1,0:T(8,128)(2,1)}), bf16[128,2048]{1,0:T(8,128)(2,1)}) %reduce-scatter.11.cloned.1.call-update) | async-done | bytes 524304 | tf_op jit(solution)/shard_map/reduce_scatter | solution.py:182
  222.3 1.4 fusion.32
  223.8 2.4 fusion.54
  226.3 7.9 %convolution_convert_fusion = bf16[1408,2048]{0,1:T(8,128)(2,1)} fusion(bf16[512,1408]{1,0:T(8,128)(2,1)} %get-tuple-element.93, bf16[512,2048]{1,0:T(8,128)(2,1)} %all-gather.9.cloned.1.call-done), kind=kOutput, calls=%fused_computation.1 | convolution fusion | flops 2955673600 | bytes 9306112 | tf_op jit(solution)/shard_map/tf,td->fd/dot_general | solution.py:177
  234.3 22.7 %all-gather.11.cloned.1.call-done = bf16[512,2048]{1,0:T(8,128)(2,1)} async-done(((bf16[128,2048]{1,0:T(8,128)(2,1)}), bf16[512,2048]{1,0:T(8,128)(2,1)}) %all-gather.11.cloned.1.call-update) | async-done | bytes 2097168 | tf_op jit(solution)/shard_map/all_gather | solution.py:201
  257.0 4.4 convolution_convert_fusion.1
  261.7 3.0 convolution_convert_fusion.4
  264.7 1.2 fusion.19
  266.0 1.0 copy.80
  267.0 4.1 multiply_reduce_fusion
  271.1 1.3 multiply_convert_fusion
  272.4 1.0 convolution_bitcast_fusion.2
  273.5 0.7 convolution_bitcast_fusion.1
  274.5 1.6 add_bitcast_fusion
  276.1 1.2 fusion.41
  277.2 1.3 copy.72
  278.8 1.5 pad_maximum_fusion.7
  280.8 7.7 %bitcast_convert_fusion = bf16[512,2048]{1,0:T(8,128)(2,1)} fusion(bf16[3,2048,512]{2,1,0:T(8,128)(2,1)} %param.11, bf16[1,512,512]{2,1,0:T(8,128)(2,1)S(1)} %copy-done.21, bf16[1,512,512]{2,1,0:T(8,128)(2,1)S(1)} %copy.79, bf16[1,512,512]{2,1,0:T(8,128)(2,1)S(1)} %copy.78), kind=kOutput, calls=%fused_computation.4 | convolution fusion | flops 3223846912 | bytes 9961472 | tf_op jit(solution)/shard_map/jtf,jdf->td/dot_general | solution.py:224
  288.8 8.1 %convolution_convert_fusion.3 = bf16[512,2048]{1,0:T(8,128)(2,1)} fusion(bf16[512,1408]{1,0:T(8,128)(2,1)} %get-tuple-element.93, bf16[1408,2048]{1,0:T(8,128)(2,1)} %param.15), kind=kOutput, calls=%fused_computation.15 | convolution fusion | flops 2953838592 | bytes 9306112 | tf_op jit(solution)/shard_map/dot_general | solution.py:168
  297.0 11.1 %convert_bitcast_fusion = bf16[2,2048,1408]{1,2,0:T(8,128)(2,1)} fusion(bf16[512,2048]{1,0:T(8,128)(2,1)} %all-gather.7.cloned.1.call-done, bf16[1,512,1408]{2,1,0:T(8,128)(2,1)} %copy-done.27, bf16[1,512,1408]{2,1,0:T(8,128)(2,1)} %copy-done.26), kind=kOutput, calls=%fused_computation | convolution fusion | flops 5912788992 | bytes 16515072 | tf_op jit(solution)/shard_map/td,jtf->jdf/dot_general | solution.py:190
  308.1 29.1 %copy.84 = bf16[2,2048,1408]{2,0,1:T(2,128)(2,1)} copy(bf16[2,2048,1408]{1,2,0:T(8,128)(2,1)} %convert_bitcast_fusion) | data formatting | bytes 23068672 | tf_op jit(solution)/shard_map/convert_element_type | solution.py:250
  337.2 7.1 %convert_bitcast_fusion.1 = bf16[3,2048,512]{1,2,0:T(8,128)(2,1)} fusion(bf16[512,2048]{1,0:T(8,128)(2,1)} %all-gather.5.cloned.1.call-done, bf16[1,512,512]{2,1,0:T(8,128)(2,1)S(1)} %copy-done.21, bf16[1,512,512]{2,1,0:T(8,128)(2,1)S(1)} %copy.79, bf16[1,512,512]{2,1,0:T(8,128)(2,1)S(1)} %copy.78), kind=kOutput, calls=%fused_computation.2 | convolution fusion | flops 3225944064 | bytes 9961472 | tf_op jit(solution)/shard_map/td,jtf->jdf/dot_general | solution.py:231
  344.3 14.1 %copy.82 = bf16[3,2048,512]{2,0,1:T(4,128)(2,1)} copy(bf16[3,2048,512]{1,2,0:T(8,128)(2,1)} %convert_bitcast_fusion.1) | data formatting | bytes 12582912 | tf_op jit(solution)/shard_map/convert_element_type | solution.py:244
  358.4 0.6 copy-done.25
  359.1 0.6 dynamic-slice.1
  360.3 1.7 convert_element_type.146
  362.0 64.4 %reduce-scatter.15.cloned.1.call-done = bf16[512,64]{0,1:T(8,128)(2,1)} async-done(((bf16[512,2048]{0,1:T(8,128)(2,1)}), bf16[512,64]{0,1:T(8,128)(2,1)}) %reduce-scatter.15.cloned.1.call-update) | async-done | bytes 65552 | tf_op jit(solution)/shard_map/reduce_scatter | solution.py:246
  426.4 1.5 convert_element_type.141
  427.9 32.0 %reduce-scatter.13.cloned.1.call-done = bf16[128,2048]{1,0:T(8,128)(2,1)} async-done(((bf16[512,2048]{1,0:T(8,128)(2,1)}), bf16[128,2048]{1,0:T(8,128)(2,1)}) %reduce-scatter.13.cloned.1.call-update) | async-done | bytes 524304 | tf_op jit(solution)/shard_map/reduce_scatter | solution.py:223
  459.9 1.4 fusion.39
  461.3 66.1 %all-reduce.2 = (f32[2048]{0:T(1024)}, f32[2048]{0:T(1024)}) all-reduce(f32[2048]{0:T(1024)S(1)} %get-tuple-element.85, f32[2048]{0:T(1024)S(1)} %get-tuple-element.83), channel_id=1, replica_groups=mesh['dp'=32,'tensor'=4] {'dp','tensor'}, use_global_device_ids=true, to_apply=%region_12.13 | all-reduce | flops 4096 | bytes 32768 | tf_op jit(solution)/shard_map/psum | solution.py:241
  527.4 3.9 fusion.27
  531.4 151.1 %all-reduce.6.cloned.1.call-done = (bf16[3,2048,512]{2,0,1:T(4,128)(2,1)}, bf16[2,2048,1408]{2,0,1:T(2,128)(2,1)}) async-done(((bf16[3,2048,512]{2,0,1:T(4,128)(2,1)}, bf16[2,2048,1408]{2,0,1:T(2,128)(2,1)}), (bf16[3,2048,512]{2,0,1:T(4,128)(2,1)}, bf16[2,2048,1408]{2,0,1:T(2,128)(2,1)})) %all-reduce.6.cloned.1.call-update) | async-done | bytes 17825808
  682.5 1.0 dynamic-slice_convert_fusion.1
  683.5 1.2 dynamic-slice_convert_fusion
  684.7 0.9 copy.85
  685.6 0.9 copy.86
  (92 shorter events, 3.7 us)
Async XLA Ops:
  7.2 63.2 %copy-start = (bf16[512,2048]{1,0:T(8,128)(2,1)S(1)}, bf16[512,2048]{1,0:T(8,128)(2,1)}, u32[]{:S(2)}) copy-start(bf16[512,2048]{1,0:T(8,128)(2,1)} %param.12) | copy-start | bytes 6291460
  7.2 37.9 %all-gather.5.cloned.1.call-start = ((), (), s32[]{:S(2)}) async-start(), calls=%async_computation.6 | async-start | bytes 2621440 | tf_op jit(solution)/shard_map/all_gather | solution.py:140
  10.7 92.4 %reduce-scatter.7.cloned.1.call-start = ((), (), s32[]{:S(2)}) async-start(), calls=%async_computation.7 | async-start | bytes 2621440 | tf_op jit(solution)/shard_map/reduce_scatter | solution.py:152
  12.5 50.7 %copy-start.14 = (f32[512,64]{1,0:T(8,128)}, f32[512,64]{1,0:T(8,128)S(1)}, u32[]{:S(2)}) copy-start(f32[512,64]{1,0:T(8,128)S(1)} %get-tuple-element.118) | copy-start | bytes 393220
  12.5 50.7 %copy-start.16 = (f32[512,64]{1,0:T(8,128)}, f32[512,64]{1,0:T(8,128)S(1)}, u32[]{:S(2)}) copy-start(f32[512,64]{1,0:T(8,128)S(1)} %get-tuple-element.119) | copy-start | bytes 393220
  51.4 16.8 %copy-start.18 = (bf16[1,512,512]{1,2,0:T(8,128)(2,1)}, bf16[1,512,512]{1,2,0:T(8,128)(2,1)S(1)}, u32[]{:S(2)}) copy-start(bf16[1,512,512]{1,2,0:T(8,128)(2,1)S(1)} %slice.93) | copy-start | bytes 1572868
  66.0 1.4 copy-start.10
  66.0 1.4 copy-start.12
  66.3 1.0 copy-start.7
  67.4 2.2 copy-start.2
  69.6 0.8 copy-start.24
  70.4 32.6 %copy-start.5 = (bf16[128,2048]{1,0:T(8,128)(2,1)S(1)}, bf16[128,2048]{1,0:T(8,128)(2,1)}, u32[]{:S(2)}) copy-start(bf16[128,2048]{1,0:T(8,128)(2,1)} %param.9) | copy-start | bytes 1572868
  73.0 31.3 %copy-start.22 = (f32[2048]{0:T(1024)S(1)}, f32[2048]{0:T(1024)}, u32[]{:S(2)}) copy-start(f32[2048]{0:T(1024)} %param.13) | copy-start | bytes 24580
  73.0 33.5 %copy-start.9 = (bf16[128,2048]{1,0:T(8,128)(2,1)S(1)}, bf16[128,2048]{1,0:T(8,128)(2,1)}, u32[]{:S(2)}) copy-start(bf16[128,2048]{1,0:T(8,128)(2,1)} %param.16) | copy-start | bytes 1572868
  73.0 64.1 %all-gather.7.cloned.1.call-start = ((), (), s32[]{:S(2)}) async-start(), calls=%async_computation.8 | async-start | bytes 2621440 | tf_op jit(solution)/shard_map/all_gather | solution.py:160
  106.4 63.9 %all-gather.9.cloned.1.call-start = ((), (), s32[]{:S(2)}) async-start(), calls=%async_computation.10 | async-start | bytes 2621440 | tf_op jit(solution)/shard_map/all_gather | solution.py:175
  107.4 114.9 %reduce-scatter.11.cloned.1.call-start = ((), (), s32[]{:S(2)}) async-start(), calls=%async_computation.11 | async-start | bytes 2621440 | tf_op jit(solution)/shard_map/reduce_scatter | solution.py:182
  180.7 1.1 copy-start.26
  180.7 1.6 copy-start.27
  182.3 40.1 %copy-start.6 = (bf16[128,2048]{1,0:T(8,128)(2,1)S(1)}, bf16[128,2048]{1,0:T(8,128)(2,1)}, u32[]{:S(2)}) copy-start(bf16[128,2048]{1,0:T(8,128)(2,1)} %reduce-scatter.7.cloned.1.call-done) | copy-start | bytes 1572868
  192.4 64.6 %all-gather.11.cloned.1.call-start = ((), (), s32[]{:S(2)}) async-start(), calls=%async_computation.12 | async-start | bytes 2621440 | tf_op jit(solution)/shard_map/all_gather | solution.py:201
  226.2 134.1 %reduce-scatter.17.cloned.1.call-start = ((), (), s32[]{:S(2)}) async-start(), calls=%async_computation.15 | async-start | bytes 5947392 | tf_op jit(solution)/shard_map/reduce_scatter | solution.py:252
  234.2 192.1 %reduce-scatter.15.cloned.1.call-start = ((), (), s32[]{:S(2)}) async-start(), calls=%async_computation.14 | async-start | bytes 2162688 | tf_op jit(solution)/shard_map/reduce_scatter | solution.py:246
  261.4 198.5 %reduce-scatter.13.cloned.1.call-start = ((), (), s32[]{:S(2)}) async-start(), calls=%async_computation.13 | async-start | bytes 2621440 | tf_op jit(solution)/shard_map/reduce_scatter | solution.py:223
  261.7 3.1 copy-start.3
  264.7 1.3 copy-start.20
  264.7 2.2 copy-start.19
  267.0 4.1 copy-start.4
  271.1 1.3 copy-start.11
  271.1 1.3 copy-start.13
  272.4 1.1 copy-start.8
  273.5 1.0 copy-start.15
  273.5 1.0 copy-start.17
  277.2 3.5 copy-start.21
  288.5 238.9 %reduce-scatter.9.cloned.1.call-start = ((), (), s32[]{:S(2)}) async-start(), calls=%async_computation.9 | async-start | bytes 2621440 | tf_op jit(solution)/shard_map/reduce_scatter | solution.py:167
  296.9 385.5 %all-reduce.6.cloned.1.call-start = ((), (), s32[]{:S(2)}) async-start(), calls=%async_computation.16 | async-start | bytes 39845888
  358.4 0.7 copy-start.25
  358.4 101.5 %copy-start.23 = (f32[2048]{0:T(1024)S(1)}, f32[2048]{0:T(1024)}, u32[]{:S(2)}) copy-start(f32[2048]{0:T(1024)} %param.10) | copy-start | bytes 24580
  527.4 159.1 %copy-start.1 = (bf16[512,2048]{1,0:T(8,128)(2,1)S(1)}, bf16[512,2048]{1,0:T(8,128)(2,1)}, u32[]{:S(2)}) copy-start(bf16[512,2048]{1,0:T(8,128)(2,1)} %param.12) | copy-start | bytes 6291460
Sparse Core Ops, SparseCore 0:
  10.8 34.2 all-gather.4
  73.2 29.8 reduce-scatter.6
  106.5 30.5 all-gather.6
  139.3 30.9 all-gather.8
  192.5 29.8 reduce-scatter.10
  226.3 30.5 all-gather.10
  260.7 83.4 reduce-scatter.16
  348.2 78.1 reduce-scatter.14
  428.9 30.9 reduce-scatter.12
  462.2 30.1 reduce-scatter.8
  496.9 185.5 all-reduce.5
where the time goes:
time: 704 us; the launch traced here: 693 us
  waiting for transfers between devices  413 us (59%)
  matrix products  101 us (14%)
  blocking collectives  66.1 us (9%)
  local copies, waits for them, and re-layouts  63.9 us (9%)
  other arithmetic  32.8 us (5%)
  between operations  16 us (2%)
    unnamed x12, waiting for transfers between devices  151 us
    psum x1, blocking collectives, body(): gain_grads = lax.psum((gain_attn_part, gain_mlp_part), ('dp', 'tensor'))  66.1 us
    reduce_scatter x1, waiting for transfers between devices, body(): lax.psum_scatter(grad_w_out.astype(jnp.bfloat16), 'dp', scatter_dimension...  64.4 us
    all_gather x1, waiting for transfers between devices, body(): whole_attn = lax.all_gather(normed_attn, 'tensor', axis=0, tiled=True)  32.6 us
    reduce_scatter x1, waiting for transfers between devices, body(): lax.psum_scatter(jnp.einsum('jtf,jdf->td', portion, w_qkv, preferred_elem...  32 us
    reduce_scatter x1, waiting for transfers between devices, body(): lax.psum_scatter(jnp.dot(context, w_out, preferred_element_type=jnp.float...  29.9 us
    reduce_scatter x1, waiting for transfers between devices, body(): lax.psum_scatter(jnp.einsum('jtf,jdf->td', portion, w_gate_up, preferred_...  29.9 us
    all_gather x1, waiting for transfers between devices, body(): whole_mlp = lax.all_gather(normed_mlp, 'tensor', axis=0, tiled=True)  29.5 us
  transfers between devices with their start and end apart: 11, of which 9 were waited for; matrix products, arithmetic and copies ran while one was open for 19% of the time, Pallas kernels for 0%

commit v1 on v0

v1 whole, which is shorter than its diff:
```python
import functools
import math

import jax
import jax.numpy as jnp
import numpy as np
from jax import lax
from jax.experimental import pallas as pl
from jax.experimental.pallas import tpu as pltpu
from jax.sharding import PartitionSpec as P

D = 2048
HD = 128
FF = 1408
ROWS = 128
SEQ = 512
HEADS = 4
EPS = 1e-05
BF = jnp.bfloat16
F32 = jnp.float32
MESH = pl.DeviceIdType.MESH
OFFS = (0, 3, 1, 2)

CX = (384, 768, 128, 384)
CY = (384, 640, 128, 384)
COLS = tuple(a + b for a, b in zip(CX, CY))
BASE = (0, 768, 2176, 2432)
ALL = 3200


def nn(a, b):
    return lax.dot_general(a, b, (((1,), (0,)), ((), ())), preferred_element_type=F32)


def nt(a, b):
    return lax.dot_general(a, b, (((1,), (1,)), ((), ())), preferred_element_type=F32)


def tn(a, b):
    return lax.dot_general(a, b, (((0,), (0,)), ((), ())), preferred_element_type=F32)


def rotary_tables():
    half = HD // 2
    freq = np.exp(np.arange(half, dtype=np.float64) * (-2.0 * math.log(10000.0) / HD))
    angles = np.arange(SEQ, dtype=np.float64)[:, None] * freq
    cos, sin = np.cos(angles), np.sin(angles)
    return (
        np.concatenate([cos, cos], axis=1).astype(np.float32),
        np.concatenate([-sin, sin], axis=1).astype(np.float32),
    )


class Place:
    def __init__(self):
        self.dp = lax.axis_index("dp")
        self.t = lax.axis_index("tensor")
        self.c = self.dp % 2
        self.x = (self.dp // 2) % 4
        self.y = self.dp // 8

    def z(self, d):
        return (self.dp, (self.t + d) % 4)

    def xs(self, d):
        return (self.y * 8 + ((self.x + d) % 4) * 2 + self.c, self.t)

    def ys(self, d):
        return (((self.y + d) % 4) * 8 + self.x * 2 + self.c, self.t)

    def core(self):
        return (self.dp + 1 - 2 * self.c, self.t)


def remote(src, dst, ssem, rsem, device):
    return pltpu.make_async_remote_copy(
        src_ref=src, dst_ref=dst, send_sem=ssem, recv_sem=rsem, device_id=device, device_id_type=MESH
    )


class Gather:
    def __init__(self, place, buf, ssem, rsem, relative):
        self.place, self.buf, self.ssem, self.rsem, self.relative = place, buf, ssem, rsem, relative

    def row(self, slot, half):
        if self.relative:
            return pl.ds(slot * 128 + half * 64, 64)
        block = (self.place.t + OFFS[slot]) % 4
        return pl.ds(pl.multiple_of(block * 128 + half * 64, 64), 64)

    def copy(self, k):
        slot, half, to, there = (
            (0, 0, 1, 1),
            (0, 1, 1, 1),
            (0, 1, -1, 2),
            (0, 0, -1, 2),
            (1, 0, 1, 3),
            (2, 1, -1, 3),
        )[k]
        src = self.buf.at[self.row(slot, half)]
        dst = self.buf.at[self.row(there, half)] if self.relative else src
        return remote(src, dst, self.ssem.at[k], self.rsem.at[k], self.place.z(to))

    def start(self):
        for k in (0, 2, 1, 3):
            self.copy(k).start()

    def relay(self):
        self.copy(0).wait_recv()
        self.copy(4).start()
        self.copy(2).wait_recv()
        self.copy(5).start()

    def near(self):
        self.copy(1).wait_recv()
        self.copy(3).wait_recv()

    def far(self):
        self.copy(4).wait_recv()
        self.copy(5).wait_recv()

    def done(self):
        for k in range(6):
            self.copy(k).wait_send()


class Scatter:
    def __init__(self, place, part, relays, recv, ssem, rsem):
        self.place, self.part, self.relays, self.recv = place, part, relays, recv
        self.ssem, self.rsem = ssem, rsem

    def rows(self, slot, half):
        return pl.ds(slot * 128 + half * 64, 64)

    def copy(self, k):
        part, relays, recv = self.part, self.relays, self.recv
        src, dst, to = (
            (part.at[self.rows(3, 0)], relays.at[0], 1),
            (part.at[self.rows(2, 1)], recv.at[0, self.rows(0, 1)], 1),
            (part.at[self.rows(3, 1)], relays.at[1], -1),
            (part.at[self.rows(1, 0)], recv.at[1, self.rows(0, 0)], -1),
            (part.at[self.rows(2, 0)], recv.at[0, self.rows(0, 0)], 1),
            (part.at[self.rows(1, 1)], recv.at[1, self.rows(0, 1)], -1),
        )[k]
        return remote(src, dst, self.ssem.at[k], self.rsem.at[k], self.place.z(to))

    def start(self, *which):
        for k in which:
            self.copy(k).start()

    def relay(self):
        for k, slot, half, out in ((0, 2, 0, 4), (2, 1, 1, 5)):
            self.copy(k).wait_recv()
            index = 0 if k == 0 else 1

            @pl.loop(0, 4)
            def _(r):
                here = pl.ds(pl.multiple_of(slot * 128 + half * 64 + r * 16, 16), 16)
                there = pl.ds(pl.multiple_of(r * 16, 16), 16)
                total = self.part[here, :].astype(F32) + self.relays[index, there, :].astype(F32)
                self.part[here, :] = total.astype(BF)

            self.copy(out).start()

    def finish(self):
        for k in (1, 3, 4, 5):
            self.copy(k).wait_recv()

    def total(self, rows):
        return (
            self.part[rows, :].astype(F32)
            + self.recv[0, rows, :].astype(F32)
            + self.recv[1, rows, :].astype(F32)
        )

    def done(self):
        for k in range(6):
            self.copy(k).wait_send()


def sixteen(r):
    return pl.ds(pl.multiple_of(r * 16, 16), 16)


def own_rows(place, r):
    return pl.ds(pl.multiple_of(place.t * 128 + r * 16, 16), 16)


def kernel(names, *refs):
    ref = dict(zip(names, refs))
    place = Place()
    tok, cot, live = ref["tok"], ref["cot"], ref["lengths"]
    wq, wo, wgu, wd = ref["wq"], ref["wo"], ref["wgu"], ref["wd"]
    attn, qkv, probs, ctx = ref["attn"], ref["qkv"], ref["probs"], ref["ctx"]
    middle, mlp, masked, branch = ref["middle"], ref["mlp"], ref["masked"], ref["branch"]
    hgg, gctx, gproj, gmid = ref["hgg"], ref["gctx"], ref["gproj"], ref["gmid"]
    cos_t, sin_t, gain1, gain2 = ref["cos"], ref["sin"], ref["gain1"], ref["gain2"]
    xa, xb = ref["xa"], [ref[f"xb{g}"] for g in range(4)]
    r1x, r1y = [ref[f"r1x{g}"] for g in range(4)], [ref[f"r1y{g}"] for g in range(4)]
    r2, final, shares = ref["r2"], ref["final"], ref["shares"]
    gacc, grecv = ref["gacc"], ref["grecv"]
    zs, zr, lsem = ref["zs"], ref["zr"], ref["lsem"]
    live_rows = live[0]

    loads = [pltpu.make_async_copy(ref["wq_h"].at[j], wq.at[j], lsem.at[j]) for j in range(3)]
    loads.append(pltpu.make_async_copy(ref["wo_h"], wo, lsem.at[3]))
    loads += [pltpu.make_async_copy(ref["wgu_h"].at[j], wgu.at[j], lsem.at[4 + j]) for j in range(2)]
    loads.append(pltpu.make_async_copy(ref["wd_h"], wd, lsem.at[6]))
    for load in loads:
        load.start()

    barrier = pltpu.get_barrier_semaphore()
    partners = [place.z(d) for d in (1, 2, 3)]
    partners += [place.xs(d) for d in (1, 2, 3)] + [place.ys(d) for d in (1, 2, 3)] + [place.core()]
    for device in partners:
        pl.semaphore_signal(barrier, inc=1, device_id=device, device_id_type=MESH)

    @pl.loop(0, 8)
    def _(r):
        v = tok[sixteen(r), :].astype(F32)
        inv = lax.rsqrt(jnp.mean(v * v, axis=-1, keepdims=True) + EPS)
        attn[own_rows(place, r), :] = (v * inv * gain1[...]).astype(BF)

    pl.semaphore_wait(barrier, len(partners))

    ag1 = Gather(place, attn, zs.at[0], zr.at[0], False)
    agm = Gather(place, masked, zs.at[1], zr.at[1], True)
    ag2 = Gather(place, mlp, zs.at[2], zr.at[2], True)
    ag4 = Gather(place, branch, zs.at[3], zr.at[3], False)
    rs1 = Scatter(place, ref["pa"], ref["relay_a"], ref["recv_a"], zs.at[4], zr.at[4])
    rs3 = Scatter(place, ref["pa"], ref["relay_a"], ref["recv_a"], zs.at[5], zr.at[5])
    rs4 = Scatter(place, ref["pa"], ref["relay_a"], ref["recv_a"], zs.at[6], zr.at[6])
    rs2 = Scatter(place, ref["pb"], ref["relay_b"], ref["recv_b"], zs.at[7], zr.at[7])

    ag1.start()

    @pl.loop(0, 8)
    def _(r):
        at = place.t * ROWS + r * 16 + lax.broadcasted_iota(jnp.int32, (16, 1), 0)
        v = cot[sixteen(r), :].astype(F32)
        masked[sixteen(r), :] = jnp.where(at < live_rows, v, 0.0).astype(BF)

    def project(slot):
        block = (place.t + OFFS[slot]) % 4
        rows = pl.ds(pl.multiple_of(block * 128, 128), 128)
        for j in range(3):
            p = nn(attn[rows, :], wq[j])
            if j == 2:
                qkv[rows, 1024:1536] = p.astype(BF)
                continue
            for h in range(HEADS):
                v = p[:, h * HD : (h + 1) * HD]
                v = v * cos_t[rows, :] + pltpu.roll(v, 64, 1) * sin_t[rows, :]
                if j == 0:
                    v = v * HD ** (-0.5)
                qkv[rows, j * 512 + h * HD : j * 512 + (h + 1) * HD] = v.astype(BF)

    for load in loads[:3]:
        load.wait()
    project(0)
    ag1.relay()
    ag1.near()
    agm.start()
    project(1)
    project(2)
    ag1.far()
    project(3)

    @pl.loop(0, HEADS)
    def _(h):
        def cols(j):
            return pl.ds(pl.multiple_of(j * 512 + h * HD, HD), HD)

        for q in range(2):
            rows, keys = pl.ds(q * 256, 256), (q + 1) * 256
            scores = nt(qkv[rows, cols(0)], qkv[0:keys, cols(1)])
            at = q * 256 + lax.broadcasted_iota(jnp.int32, (256, keys), 0)
            key = lax.broadcasted_iota(jnp.int32, (256, keys), 1)
            scores = jnp.where((key <= at) & (key < live_rows), scores, -1e30)
            e = jnp.exp(scores - jnp.max(scores, axis=-1, keepdims=True))
            p = (e * (1.0 / jnp.sum(e, axis=-1, keepdims=True))).astype(BF)
            probs[h, rows, 0:keys] = p
            ctx[rows, cols(0)] = nn(p, qkv[0:keys, cols(2)]).astype(BF)

    agm.relay()
    loads[3].wait()

    def out_part(slot):
        block = (place.t + OFFS[slot]) % 4
        rows = pl.ds(pl.multiple_of(block * 128, 128), 128)

        @pl.loop(0, 4)
        def _(n):
            at = pl.ds(pl.multiple_of(n * 512, 512), 512)
            rs1.part[slot * 128 : (slot + 1) * 128, at] = nn(ctx[rows, :], wo[:, at]).astype(BF)

    out_part(3)
    rs1.start(0, 2)
    out_part(2)
    rs1.start(1)
    out_part(1)
    rs1.start(3)
    out_part(0)

    other = 1 - place.c
    xs, xr = ref["xs"], ref["xr"]

    def half(group):
        if group == 0:
            return hgg.at[0, :, pl.ds(pl.multiple_of(other * 640, 128), 768)]
        if group == 1:
            return hgg.at[1 + other]
        if group == 2:
            return ctx.at[:, pl.ds(pl.multiple_of(other * 256, 256), 256)]
        return gproj.at[:, pl.ds(pl.multiple_of(other * 768, 256), 768)]

    def swap_a(group):
        src = (masked, mlp, branch, attn)[group]
        return remote(src, xa.at[group], xs.at[group], xr.at[group], place.core())

    def swap_b(group):
        return remote(half(group), xb[group], xs.at[4 + group], xr.at[4 + group], place.core())

    swap_a(3).start()
    swap_b(2).start()

    rs1.relay()
    agm.near()
    agm.far()
    swap_a(0).start()
    rs1.finish()

    @pl.loop(0, 8)
    def _(r):
        rows = sixteen(r)
        v = tok[rows, :].astype(F32) + rs1.total(rows)
        middle[rows, :] = v
        inv = lax.rsqrt(jnp.mean(v * v, axis=-1, keepdims=True) + EPS)
        mlp[rows, :] = (v * inv * gain2[...]).astype(BF)

    rs1.done()
    ag2.start()
    for load in loads[4:]:
        load.wait()

    def feed(first, count):
        rows = slice(first, first + count)
        for n0, n1 in ((0, 512), (512, 1024), (1024, 1408)):
            gate = nn(mlp[rows, :], wgu[0, :, n0:n1])
            up = nn(mlp[rows, :], wgu[1, :, n0:n1])
            grad = nt(masked[rows, :], wd[n0:n1, :])
            sig = jax.nn.sigmoid(gate)
            silu = gate * sig
            hgg[0, rows, n0:n1] = (silu * up).astype(BF)
            hgg[1, rows, n0:n1] = (grad * up * sig * (1.0 + gate * (1.0 - sig))).astype(BF)
            hgg[2, rows, n0:n1] = (grad * silu).astype(BF)

        @pl.loop(0, 4)
        def _(n):
            at = pl.ds(pl.multiple_of(n * 512, 512), 512)
            part = nt(hgg[1, rows, :], wgu[0, at, :]) + nt(hgg[2, rows, :], wgu[1, at, :])
            rs3.part[rows, at] = part.astype(BF)

    feed(0, 128)
    ag2.relay()
    ag2.near()
    feed(128, 256)
    rs3.start(1, 3)
    ag2.far()
    feed(384, 128)
    rs3.start(0, 2)
    swap_a(1).start()
    swap_b(0).start()
    swap_b(1).start()

    @pl.loop(0, 4)
    def _(n):
        at = pl.ds(pl.multiple_of(n * 512, 512), 512)
        rs2.part[:, at] = nn(hgg[0], wd[:, at]).astype(BF)

    rs3.relay()
    rs2.start(0, 2, 1, 3)

    own_b = (
        hgg.at[0, :, pl.ds(pl.multiple_of(place.c * 640, 128), 768)],
        hgg.at[1 + place.c],
        ctx.at[:, pl.ds(pl.multiple_of(place.c * 256, 256), 256)],
        gproj.at[:, pl.ds(pl.multiple_of(place.c * 768, 256), 768)],
    )
    own_a = (masked, mlp, branch, attn)
    other_a = (wd.at[0:512], wd.at[512:1024], wd.at[0:512], wd.at[512:1024])
    other_b = (wgu.at[0, 0:512, 0:768], ref["pa"].at[:, 0:1408], hgg.at[1, :, 0:256], hgg.at[0, :, 0:768])
    osem = ref["osem"]

    def bring(group):
        return (
            pltpu.make_async_copy(xa.at[group], other_a[group], osem.at[group]),
            pltpu.make_async_copy(xb[group], other_b[group], osem.at[4 + group]),
        )

    def piece(group, axis, tile, first, count):
        if group == 3 and axis == 1:
            return mlp.at[pl.ds(first, count), pl.ds(pl.multiple_of(tile * 384, 128), 384)]
        plane, base = ((1, 0), (0, 0), (1, 768), (1, 1024))[group]
        lo = base if axis == 0 else base + CX[group]
        width = CX[group] if axis == 0 else CY[group]
        rows = pl.ds(pl.multiple_of(tile * 512 + first, 128), count)
        return wgu.at[plane, rows, lo : lo + width]

    p1xs, p1xr, p1ys, p1yr = ref["p1xs"], ref["p1xr"], ref["p1ys"], ref["p1yr"]

    def send_x(group, d, tile):
        first = pl.multiple_of(((place.x + d) % 4) * 128, 128)
        dst = r1x[group].at[d - 1, pl.ds(pl.multiple_of(tile * 128, 128), 128)]
        sem = (group * 3 + d - 1) * 4 + tile
        return remote(piece(group, 0, tile, first, 128), dst, p1xs.at[sem], p1xr.at[sem], place.xs(d))

    def send_y(group, d):
        sem = group * 3 + d - 1
        src = piece(group, 1, (place.y + d) % 4, 0, 512)
        return remote(src, r1y[group].at[d - 1], p1ys.at[sem], p1yr.at[sem], place.ys(d))

    def gradient(group, step):
        tile = (place.y + 1 + step) % 4
        at = pl.ds(pl.multiple_of(tile * 512, 512), 512)
        lo = 0
        for axis, width in ((0, CX[group]), (1, CY[group])):
            own, oth = own_b[group].at[:, lo : lo + width], other_b[group].at[:, lo : lo + width]
            out = tn(own_a[group][:, at], own[...]) + tn(other_a[group][:, at], oth[...])
            piece(group, axis, tile, 0, 512)[...] = out.astype(BF)
            lo += width
        for d in (1, 2, 3):
            send_x(group, d, tile).start()

            @pl.when(step == d - 1)
            def _():
                send_y(group, d).start()

    def fetch(group):
        swap_a(group).wait_recv()
        swap_b(group).wait_recv()
        for copy in bring(group):
            copy.start()

    def fetched(group):
        for copy in bring(group):
            copy.wait()

    fetch(0)
    fetched(0)

    @pl.loop(0, 4)
    def _(step):
        gradient(0, step)

    rs3.finish()

    def fold(v):
        return jnp.concatenate([v[:, i * 512 : (i + 1) * 512] for i in range(4)], axis=0)

    def mlp_back(r, total):
        rows = sixteen(r)
        grad = rs3.total(rows)
        v = middle[rows, :]
        inv = lax.rsqrt(jnp.mean(v * v, axis=-1, keepdims=True) + EPS)
        scaled = grad * gain2[...]
        back = (
            masked[rows, :].astype(F32)
            + inv * scaled
            - v * (inv * inv * inv) * jnp.mean(v * scaled, axis=-1, keepdims=True)
        )
        gmid[rows, :] = back
        branch[own_rows(place, r), :] = back.astype(BF)
        return total + jnp.sum(grad * v * inv, axis=0, keepdims=True)

    gain2_part = lax.fori_loop(0, 8, mlp_back, jnp.zeros((1, D), F32))
    gacc[0, 4:8, :] = fold(gain2_part)
    ag4.start()
    rs3.done()
    fetch(1)
    rs2.relay()
    fetched(1)

    @pl.loop(0, 2)
    def _(step):
        gradient(1, step)

    ag4.relay()

    @pl.loop(2, 4)
    def _(step):
        gradient(1, step)

    ag4.near()
    ag4.far()
    swap_a(2).start()

    @pl.loop(0, 2)
    def _(n):
        at = pl.ds(pl.multiple_of(n * 256, 256), 256)
        gctx[:, at] = nt(branch[...], wo[at, :]).astype(BF)

    def turn_back(v, rows):
        return v * cos_t[rows, :] - pltpu.roll(v, 64, 1) * sin_t[rows, :]

    @pl.loop(0, HEADS)
    def _(h):
        def cols(j):
            return pl.ds(pl.multiple_of(j * 512 + h * HD, HD), HD)

        def part(q):
            rows, keys = pl.ds(q * 256, 256), (q + 1) * 256
            p = probs[h, rows, 0:keys]
            grad = gctx[rows, cols(0)]
            wide = p.astype(F32)
            gp = nt(grad, qkv[0:keys, cols(2)])
            gs = (wide * (gp - jnp.sum(wide * gp, axis=-1, keepdims=True))).astype(BF)
            gq = nn(gs, qkv[0:keys, cols(1)])
            gproj[rows, cols(0)] = (turn_back(gq, rows) * HD ** (-0.5)).astype(BF)
            return tn(gs, qkv[rows, cols(0)]), tn(p, grad)

        k1, v1 = part(1)
        k0, v0 = part(0)
        lo, hi = slice(0, 256), slice(256, 512)
        gproj[lo, cols(1)] = turn_back(k0 + k1[lo], lo).astype(BF)
        gproj[hi, cols(1)] = turn_back(k1[hi], hi).astype(BF)
        gproj[lo, cols(2)] = (v0 + v1[lo]).astype(BF)
        gproj[hi, cols(2)] = v1[hi].astype(BF)

    swap_b(3).start()

    def attn_part(slot):
        block = (place.t + OFFS[slot]) % 4
        rows = pl.ds(pl.multiple_of(block * 128, 128), 128)

        @pl.loop(0, 4)
        def _(n):
            at = pl.ds(pl.multiple_of(n * 512, 512), 512)
            part = nt(gproj[rows, 0:512], wq[0, at, :])
            for j in (1, 2):
                part = part + nt(gproj[rows, j * 512 : (j + 1) * 512], wq[j, at, :])
            rs4.part[slot * 128 : (slot + 1) * 128, at] = part.astype(BF)

    attn_part(3)
    rs4.start(0, 2)
    attn_part(2)
    rs4.start(1)
    attn_part(1)
    rs4.start(3)
    attn_part(0)

    rs2.finish()

    @pl.loop(0, 8)
    def _(r):
        rows = sixteen(r)
        middle[rows, :] = middle[rows, :] + rs2.total(rows)

    out_copy = pltpu.make_async_copy(middle, ref["output"], lsem.at[7])
    out_copy.start()
    rs4.relay()

    swap_a(1).wait_send()
    swap_b(0).wait_send()
    swap_b(1).wait_send()
    ag2.done()
    for group in (3, 2):
        fetch(group)
    for group in (3, 2):
        fetched(group)

        @pl.loop(0, 4)
        def _(step):
            gradient(group, step)

    rs4.finish()

    def attn_back(r, total):
        rows = sixteen(r)
        grad = rs4.total(rows)
        v = tok[rows, :].astype(F32)
        inv = lax.rsqrt(jnp.mean(v * v, axis=-1, keepdims=True) + EPS)
        scaled = grad * gain1[...]
        gmid[rows, :] = (
            gmid[rows, :]
            + inv * scaled
            - v * (inv * inv * inv) * jnp.mean(v * scaled, axis=-1, keepdims=True)
        )
        return total + jnp.sum(grad * v * inv, axis=0, keepdims=True)

    gain1_part = lax.fori_loop(0, 8, attn_back, jnp.zeros((1, D), F32))
    gacc[0, 0:4, :] = fold(gain1_part)
    tok_copy = pltpu.make_async_copy(gmid, ref["grad_tokens"], lsem.at[8])
    tok_copy.start()

    gs, gr = ref["gs"], ref["gr"]

    def spread(stage):
        count = 2 if stage == 3 else 4
        me = (place.t, place.x, place.y, place.c)[stage]
        out = []
        for d in range(1, count):
            device = (place.z, place.xs, place.ys, lambda _: place.core())[stage](d)
            k = stage * 3 + d - 1
            out.append(remote(gacc.at[stage], grecv.at[stage * 4 + me], gs.at[k], gr.at[k], device))
        return out, count, me

    def spread_start(stage):
        copies, _, me = spread(stage)
        grecv[stage * 4 + me] = gacc[stage]
        for copy in copies:
            copy.start()

    def spread_end(stage):
        copies, count, _ = spread(stage)
        for copy in copies:
            copy.wait_recv()
        total = grecv[stage * 4]
        for i in range(1, count):
            total = total + grecv[stage * 4 + i]
        gacc[stage + 1] = total

    spread_start(0)

    lands = ref["lands"]
    p2xs, p2xr, p2ys, p2yr = ref["p2xs"], ref["p2xr"], ref["p2ys"], ref["p2yr"]

    def landing(group, axis, d):
        if axis == 0:
            src, dst = r1x[group], hgg.at[d - 1, :, 0 : CX[group]]
        else:
            src, dst = r1y[group], hgg.at[d - 1, :, 768 : 768 + CY[group]]
        return pltpu.make_async_copy(src.at[d - 1], dst, lands.at[(group * 2 + axis) * 3 + d - 1])

    def send_2(group, axis, d):
        sem = group * 3 + d - 1
        own = pl.multiple_of(place.x * 128, 128)
        if axis == 0:
            src = piece(group, 0, (place.y + d) % 4, own, 128)
            dst = r2.at[d - 1, :, BASE[group] : BASE[group] + CX[group]]
            return remote(src, dst, p2xs.at[sem], p2xr.at[sem], place.ys(d))
        src = piece(group, 1, place.y, pl.multiple_of(((place.x + d) % 4) * 128, 128), 128)
        dst = r2.at[d - 1, :, BASE[group] + CX[group] : BASE[group] + COLS[group]]
        return remote(src, dst, p2ys.at[sem], p2yr.at[sem], place.xs(d))

    def land(group):
        for d in (1, 2, 3):
            for tile in range(4):
                send_x(group, d, tile).wait_recv()
            landing(group, 0, d).start()
        for d in (1, 2, 3):
            send_y(group, d).wait_recv()
            landing(group, 1, d).start()

    def first_sum(group):
        for axis in range(2):
            for d in (1, 2, 3):
                landing(group, axis, d).wait()
            lo = 0 if axis == 0 else 768
            width = CX[group] if axis == 0 else CY[group]

            @pl.loop(0, 4)
            def _(i):
                if axis == 0:
                    own = piece(group, 0, i, pl.multiple_of(place.x * 128, 128), 128)
                else:
                    own = piece(group, 1, place.y, pl.multiple_of(i * 128, 128), 128)
                rows = pl.ds(pl.multiple_of(i * 128, 128), 128)
                total = own[...].astype(F32)
                for d in range(3):
                    total = total + hgg[d, rows, lo : lo + width].astype(F32)
                own[...] = total.astype(BF)

            for d in (1, 2, 3):
                send_2(group, axis, d).start()

    def second_sum(group):
        own = pl.multiple_of(place.x * 128, 128)
        for axis in range(2):
            for d in (1, 2, 3):
                send_2(group, axis, d).wait_recv()
            lo = BASE[group] + (0 if axis == 0 else CX[group])
            width = CX[group] if axis == 0 else CY[group]
            total = piece(group, axis, place.y, own, 128)[...].astype(F32)
            for d in range(3):
                total = total + r2[d, :, lo : lo + width].astype(F32)
            final[:, lo : lo + width] = total

    land(0)
    first_sum(0)
    spread_end(0)
    spread_start(1)
    land(1)
    first_sum(1)
    spread_end(1)
    spread_start(2)
    second_sum(0)
    land(2)
    first_sum(2)
    spread_end(2)
    spread_start(3)
    land(3)
    first_sum(3)
    second_sum(1)
    spread_end(3)
    ref["gains"][...] = gacc[4]
    second_sum(2)
    second_sum(3)

    mine = final.at[pl.ds(pl.multiple_of(place.c * 64, 64), 64)]
    theirs = final.at[pl.ds(pl.multiple_of(other * 64, 64), 64)]
    last = remote(theirs, shares.at[place.c], xs.at[8], xr.at[8], place.core())
    last.start()
    keep = pltpu.make_async_copy(mine, shares.at[place.c], lsem.at[9])
    keep.start()

    for gather in (ag1, agm, ag4):
        gather.done()
    rs4.done()
    rs2.done()
    for group in (0, 2, 3):
        swap_a(group).wait_send()
    for group in (2, 3):
        swap_b(group).wait_send()
    for group in range(4):
        for d in (1, 2, 3):
            for tile in range(4):
                send_x(group, d, tile).wait_send()
            send_y(group, d).wait_send()
            for axis in range(2):
                send_2(group, axis, d).wait_send()
    for stage in range(4):
        for copy in spread(stage)[0]:
            copy.wait_send()
    out_copy.wait()
    tok_copy.wait()
    keep.wait()
    last.wait()


def block(tokens, gain_attn, w_qkv, w_out, gain_mlp, w_gate_up, w_down, cotangent, lengths):
    cos_t, sin_t = rotary_tables()
    vmem = pl.BlockSpec(memory_space=pltpu.VMEM)
    smem = pl.BlockSpec(memory_space=pltpu.SMEM)
    hbm = pl.BlockSpec(memory_space=pl.ANY)
    ins = [
        ("tok", tokens, vmem),
        ("gain1", gain_attn.reshape(1, D), vmem),
        ("wq_h", w_qkv, hbm),
        ("wo_h", w_out, hbm),
        ("gain2", gain_mlp.reshape(1, D), vmem),
        ("wgu_h", w_gate_up, hbm),
        ("wd_h", w_down, hbm),
        ("cot", cotangent, vmem),
        ("lengths", lengths, smem),
        ("cos", jnp.asarray(cos_t), vmem),
        ("sin", jnp.asarray(sin_t), vmem),
    ]
    outs = [
        ("output", (ROWS, D), F32, hbm),
        ("grad_tokens", (ROWS, D), F32, hbm),
        ("gains", (8, 512), F32, vmem),
        ("shares", (2, 64, ALL), F32, hbm),
        ("xa", (4, SEQ, D), BF, hbm),
    ]
    outs += [(f"xb{g}", (SEQ, COLS[g]), BF, hbm) for g in range(4)]
    outs += [(f"r1x{g}", (3, SEQ, CX[g]), BF, hbm) for g in range(4)]
    outs += [(f"r1y{g}", (3, SEQ, CY[g]), BF, hbm) for g in range(4)]
    dma = pltpu.SemaphoreType.DMA
    scratch = [
        ("wq", pltpu.VMEM((3, D, 512), BF)),
        ("wo", pltpu.VMEM((512, D), BF)),
        ("wgu", pltpu.VMEM((2, D, FF), BF)),
        ("wd", pltpu.VMEM((FF, D), BF)),
        ("attn", pltpu.VMEM((SEQ, D), BF)),
        ("qkv", pltpu.VMEM((SEQ, 1536), BF)),
        ("probs", pltpu.VMEM((HEADS, SEQ, SEQ), BF)),
        ("ctx", pltpu.VMEM((SEQ, 512), BF)),
        ("middle", pltpu.VMEM((ROWS, D), F32)),
        ("mlp", pltpu.VMEM((SEQ, D), BF)),
        ("masked", pltpu.VMEM((SEQ, D), BF)),
        ("branch", pltpu.VMEM((SEQ, D), BF)),
        ("hgg", pltpu.VMEM((3, SEQ, FF), BF)),
        ("gctx", pltpu.VMEM((SEQ, 512), BF)),
        ("gproj", pltpu.VMEM((SEQ, 1536), BF)),
        ("gmid", pltpu.VMEM((ROWS, D), F32)),
        ("pa", pltpu.VMEM((SEQ, D), BF)),
        ("relay_a", pltpu.VMEM((2, 64, D), BF)),
        ("recv_a", pltpu.VMEM((2, ROWS, D), BF)),
        ("pb", pltpu.VMEM((SEQ, D), BF)),
        ("relay_b", pltpu.VMEM((2, 64, D), BF)),
        ("recv_b", pltpu.VMEM((2, ROWS, D), BF)),
        ("r2", pltpu.VMEM((3, ROWS, ALL), BF)),
        ("final", pltpu.VMEM((ROWS, ALL), F32)),
        ("gacc", pltpu.VMEM((5, 8, 512), F32)),
        ("grecv", pltpu.VMEM((14, 8, 512), F32)),
        ("zs", dma((8, 6))),
        ("zr", dma((8, 6))),
        ("lsem", dma((10,))),
        ("osem", dma((8,))),
        ("xs", dma((9,))),
        ("xr", dma((9,))),
        ("p1xs", dma((48,))),
        ("p1xr", dma((48,))),
        ("p1ys", dma((12,))),
        ("p1yr", dma((12,))),
        ("p2xs", dma((12,))),
        ("p2xr", dma((12,))),
        ("p2ys", dma((12,))),
        ("p2yr", dma((12,))),
        ("lands", dma((24,))),
        ("gs", dma((10,))),
        ("gr", dma((10,))),
    ]
    names = [i[0] for i in ins] + [o[0] for o in outs] + [s[0] for s in scratch]
    results = pl.pallas_call(
        functools.partial(kernel, names),
        out_shape=[jax.ShapeDtypeStruct(o[1], o[2]) for o in outs],
        in_specs=[i[2] for i in ins],
        out_specs=[o[3] for o in outs],
        scratch_shapes=[s[1] for s in scratch],
        compiler_params=pltpu.CompilerParams(
            collective_id=0, has_side_effects=True, vmem_limit_bytes=63 * 1024 * 1024
        ),
        name="block",
    )(*[i[1] for i in ins])
    output, grad_tokens, gains, shares = results[:4]
    gains = gains.reshape(2, D)
    b = BASE
    down = jnp.concatenate([shares[0, :, 0:768], shares[1, :, 128:768]], axis=1)
    gate_up = shares[:, :, b[1] : b[1] + FF]
    out = jnp.concatenate([shares[0, :, b[2] : b[2] + 256], shares[1, :, b[2] : b[2] + 256]], axis=1)
    qkv = jnp.concatenate([shares[0, :, b[3] :], shares[1, :, b[3] :]], axis=1)
    return (
        output,
        grad_tokens,
        gains[0],
        qkv.reshape(64, 3, 512).transpose(1, 0, 2),
        out.T,
        gains[1],
        gate_up,
        down.T,
    )


def solution(mesh):
    placed = (
        P(("dp", "tensor"), None),
        P(),
        P(None, None, "tensor"),
        P("tensor", None),
        P(),
        P(None, None, "tensor"),
        P("tensor", None),
        P(("dp", "tensor"), None),
        P("dp"),
    )
    return jax.shard_map(
        block,
        mesh=mesh,
        in_specs=placed,
        out_specs=(
            P(("dp", "tensor"), None),
            P(("dp", "tensor"), None),
            P(),
            P(None, "dp", "tensor"),
            P("tensor", "dp"),
            P(),
            P(None, "dp", "tensor"),
            P("tensor", "dp"),
        ),
        check_vma=False,
    )
```

time: 704 us -> 224 us (0.32); the launches traced: 693 us -> 223 us
  waiting for transfers between devices: 413 us -> 0 us
  Pallas kernels: 0 us -> 211 us
  matrix products: 101 us -> 0 us
  blocking collectives: 66.1 us -> 0 us
  local copies, waits for them, and re-layouts: 63.9 us -> 10.1 us
  other arithmetic: 32.8 us -> 1.45 us
  between operations: 16 us -> 1.33 us
    pallas_call x0 -> x1, Pallas kernels: none -> 211 us  [block(): pl.pallas_call(functools.partial(kernel, names), out_shape=[jax.ShapeDtyp...]
    reduce_scatter x6 -> x0, waiting for transfers between devices: 156 us -> none  [the longest x1 64.4 us: body(): lax.psum_scatter(grad_w_out.astype(jnp.bfloat16), 'dp', scatter_dimension...]
    unnamed x12 -> x0, waiting for transfers between devices: 151 us -> none
    all_gather x4 -> x0, waiting for transfers between devices: 105 us -> none  [the longest x1 32.6 us: body(): whole_attn = lax.all_gather(normed_attn, 'tensor', axis=0, tiled=True)]
    dot_general x18 -> x0, matrix products: 101 us -> none  [the longest x1 12.6 us: body(): jnp.einsum('td,jdf->jtf', whole_mlp, w_gate_up, preferred_element_type=jn...]
    psum x1 -> x0, blocking collectives: 66.1 us -> none  [body(): gain_grads = lax.psum((gain_attn_part, gain_mlp_part), ('dp', 'tensor'))]
    convert_element_type x2 -> x0, local copies, waits for them, and re-layouts: 43.2 us -> none  [the longest x1 29.1 us: body(): grad_w_gate_up.astype(jnp.bfloat16)]
    convert_element_type x10 -> x0, other arithmetic: 13.5 us -> none  [the longest x4 5.42 us: body(): shares = (lax.psum_scatter(grad_w_qkv.astype(jnp.bfloat16), 'dp', scatter...]
  transfers between devices with their start and end apart: 11 -> 0, of which waited for: 9 -> 0; matrix products, arithmetic and copies ran while one was open for 19% -> 0% of each run, Pallas kernels for 0% -> 0%
where the time goes in v1:
time: 224 us; the launch traced here: 223 us
  Pallas kernels  211 us (94%)
  local copies, waits for them, and re-layouts  10.1 us (5%)
    pallas_call x1, Pallas kernels, block(): pl.pallas_call(functools.partial(kernel, names), out_shape=[jax.ShapeDtyp...  211 us
    unnamed x10, local copies, waits for them, and re-layouts  4.82 us

profile of v1, /device:TPU:1, one launch (start us, length us, event | category | flops | bytes accessed | tf_op | source)
XLA Modules:
  0.0 223.5 jit_solution(5584737754592415141)
XLA Ops:
  1.3 210.6 %block.1 = (f32[128,2048]{1,0:T(8,128)}, f32[128,2048]{1,0:T(8,128)}, f32[8,512]{1,0:T(8,128)}, f32[2,64,3200]{2,1,0:T(8,128)}, bf16[4,512,2048]{2,1,0:T(8,128)(...) custom-call(bf16[128,2048]{1,0:T(8,128)(2,1)} %refs_0_.1, ...), custom_call_target="tpu_custom_call" | custom-call | tf_op jit(solution)/shard_map/block/pallas_call | solution.py:816
  211.9 0.8 slice_bitcast_fusion.6
  212.7 0.6 copy.22
  213.3 0.6 copy.21
  213.9 0.9 slice_bitcast_fusion.5
  214.8 0.7 maximum_bitcast_fusion.1
  215.5 0.9 slice_bitcast_fusion.3
  216.4 1.2 slice_bitcast_fusion
  217.6 2.0 slice.35
  219.6 0.0 copy-start.1
  219.6 0.8 maximum_bitcast_fusion
  220.4 0.3 reshape.32
  220.6 0.0 copy-start
  220.7 0.9 copy.20
  221.5 0.0 copy-done.1
  221.5 1.0 copy.26
  222.5 0.0 copy-done
  222.5 1.0 copy.27
  (1 shorter events, 0.0 us)
Async XLA Ops:
  219.6 2.0 copy-start.1
  220.6 1.9 copy-start

commit v2 on v1

v2 whole, which is shorter than its diff:
```python
import functools
import math

import jax
import jax.numpy as jnp
import numpy as np
from jax import lax
from jax.experimental import pallas as pl
from jax.experimental.pallas import tpu as pltpu
from jax.sharding import PartitionSpec as P

D = 2048
HD = 128
FF = 1408
ROWS = 128
SEQ = 512
HEADS = 4
EPS = 1e-05
BF = jnp.bfloat16
F32 = jnp.float32
MESH = pl.DeviceIdType.MESH
OFFS = (0, 3, 1, 2)
ORDER = ((0, 0), (0, 1), (1, 0), (2, 1), (1, 1), (2, 0), (3, 0), (3, 1))
UNIT = {half: i * 64 for i, half in enumerate(ORDER)}

CX = (384, 768, 128, 384)
CY = (384, 640, 128, 384)
COLS = tuple(a + b for a, b in zip(CX, CY))
BASE = (0, 768, 2176, 2432)
ALL = 3200


def nn(a, b):
    return lax.dot_general(a, b, (((1,), (0,)), ((), ())), preferred_element_type=F32)


def nt(a, b):
    return lax.dot_general(a, b, (((1,), (1,)), ((), ())), preferred_element_type=F32)


def tn(a, b):
    return lax.dot_general(a, b, (((0,), (0,)), ((), ())), preferred_element_type=F32)


def rotary_tables():
    half = HD // 2
    freq = np.exp(np.arange(half, dtype=np.float64) * (-2.0 * math.log(10000.0) / HD))
    angles = np.arange(SEQ, dtype=np.float64)[:, None] * freq
    cos, sin = np.cos(angles), np.sin(angles)
    return (
        np.concatenate([cos, cos], axis=1).astype(np.float32),
        np.concatenate([-sin, sin], axis=1).astype(np.float32),
    )


class Place:
    def __init__(self):
        self.dp = lax.axis_index("dp")
        self.t = lax.axis_index("tensor")
        self.c = self.dp % 2
        self.x = (self.dp // 2) % 4
        self.y = self.dp // 8

    def z(self, d):
        return (self.dp, (self.t + d) % 4)

    def xs(self, d):
        return (self.y * 8 + ((self.x + d) % 4) * 2 + self.c, self.t)

    def ys(self, d):
        return (((self.y + d) % 4) * 8 + self.x * 2 + self.c, self.t)

    def core(self):
        return (self.dp + 1 - 2 * self.c, self.t)


def remote(src, dst, ssem, rsem, device):
    return pltpu.make_async_remote_copy(
        src_ref=src, dst_ref=dst, send_sem=ssem, recv_sem=rsem, device_id=device, device_id_type=MESH
    )


def half_rows(place, slot, half):
    block = (place.t + OFFS[slot]) % 4
    return pl.ds(pl.multiple_of(block * 128 + half * 64, 64), 64)


def in_order(place, ref, cols):
    return jnp.concatenate([ref[half_rows(place, *half), cols] for half in ORDER], axis=0)


class Gather:
    def __init__(self, place, buf, ssem, rsem, relative):
        self.place, self.buf, self.ssem, self.rsem, self.relative = place, buf, ssem, rsem, relative

    def row(self, slot, half):
        if self.relative:
            return pl.ds(UNIT[slot, half], 64)
        return half_rows(self.place, slot, half)

    def copy(self, k):
        slot, half, to, there = (
            (0, 0, 1, 1),
            (0, 1, 1, 1),
            (0, 1, -1, 2),
            (0, 0, -1, 2),
            (1, 0, 1, 3),
            (2, 1, -1, 3),
        )[k]
        src = self.buf.at[self.row(slot, half)]
        dst = self.buf.at[self.row(there, half)] if self.relative else src
        return remote(src, dst, self.ssem.at[k], self.rsem.at[k], self.place.z(to))

    def start(self):
        for k in (0, 2, 1, 3):
            self.copy(k).start()

    def relay(self):
        self.copy(0).wait_recv()
        self.copy(4).start()
        self.copy(2).wait_recv()
        self.copy(5).start()

    def near(self):
        self.copy(1).wait_recv()
        self.copy(3).wait_recv()

    def far(self):
        self.copy(4).wait_recv()
        self.copy(5).wait_recv()

    def done(self):
        for k in range(6):
            self.copy(k).wait_send()


class Scatter:
    def __init__(self, place, part, relays, recv, ssem, rsem):
        self.place, self.part, self.relays, self.recv = place, part, relays, recv
        self.ssem, self.rsem = ssem, rsem

    def rows(self, slot, half):
        return pl.ds(UNIT[slot, half], 64)

    def copy(self, k, n):
        part, relays, recv = self.part, self.relays, self.recv
        cols = pl.ds(pl.multiple_of(n * 512, 512), 512)
        src, dst, to = (
            (part.at[self.rows(3, 0), cols], relays.at[0, :, cols], 1),
            (part.at[self.rows(2, 1), cols], recv.at[0, self.rows(0, 1), cols], 1),
            (part.at[self.rows(3, 1), cols], relays.at[1, :, cols], -1),
            (part.at[self.rows(1, 0), cols], recv.at[1, self.rows(0, 0), cols], -1),
            (part.at[self.rows(2, 0), cols], recv.at[0, self.rows(0, 0), cols], 1),
            (part.at[self.rows(1, 1), cols], recv.at[1, self.rows(0, 1), cols], -1),
        )[k]
        sem = k * 4 + n
        return remote(src, dst, self.ssem.at[sem], self.rsem.at[sem], self.place.z(to))

    def start(self, n, *which):
        for k in which:
            self.copy(k, n).start()

    def relay(self, first, last):
        @pl.loop(first, last)
        def _(n):
            cols = pl.ds(pl.multiple_of(n * 512, 512), 512)
            for index, slot, half, out in ((0, 2, 0, 4), (1, 1, 1, 5)):
                self.copy(2 * index, n).wait_recv()
                rows = self.rows(slot, half)
                total = self.part[rows, cols].astype(F32) + self.relays[index, :, cols].astype(F32)
                self.part[rows, cols] = total.astype(BF)
                self.copy(out, n).start()

    def finish(self):
        @pl.loop(0, 4)
        def _(n):
            for k in (1, 3, 4, 5):
                self.copy(k, n).wait_recv()

    def total(self, rows):
        return (
            self.part[rows, :].astype(F32)
            + self.recv[0, rows, :].astype(F32)
            + self.recv[1, rows, :].astype(F32)
        )

    def done(self):
        @pl.loop(0, 4)
        def _(n):
            for k in range(6):
                self.copy(k, n).wait_send()


def sixteen(r):
    return pl.ds(pl.multiple_of(r * 16, 16), 16)


def own_rows(place, r):
    return pl.ds(pl.multiple_of(place.t * 128 + r * 16, 16), 16)


def kernel(names, *refs):
    ref = dict(zip(names, refs))
    place = Place()
    tok, cot, live = ref["tok"], ref["cot"], ref["lengths"]
    wq, wo, wgu, wd = ref["wq"], ref["wo"], ref["wgu"], ref["wd"]
    attn, qkv, probs, ctx = ref["attn"], ref["qkv"], ref["probs"], ref["ctx"]
    middle, mlp, masked, branch = ref["middle"], ref["mlp"], ref["masked"], ref["branch"]
    hid, ggu, gctx, gproj, gmid = ref["hid"], ref["ggu"], ref["gctx"], ref["qkv"], ref["gmid"]
    cos_t, sin_t, gain1, gain2 = ref["cos"], ref["sin"], ref["gain1"], ref["gain2"]
    xa, xa0, xb0, xb1, xb2 = ref["xa"], ref["xa0"], ref["xb0"], ref["xb1"], ref["xb2"]
    relx, rely = [ref[f"relx{g}"] for g in range(4)], [ref[f"rely{g}"] for g in range(4)]
    recx, recy = [ref[f"recx{g}"] for g in range(4)], [ref[f"recy{g}"] for g in range(4)]
    r2, final, shares = ref["r2"], ref["final"], ref["shares"]
    gacc, grecv, gsum = ref["gacc"], ref["grecv"], ref["gsum"]
    zs, zr, lsem = ref["zs"], ref["zr"], ref["lsem"]
    live_rows = live[0]

    cot_load = pltpu.make_async_copy(cot, masked.at[0:ROWS], lsem.at[7])
    cot_load.start()

    loads = [pltpu.make_async_copy(ref["wq_h"].at[j], wq.at[:, j * 512 : (j + 1) * 512], lsem.at[j]) for j in range(3)]
    loads.append(pltpu.make_async_copy(ref["wo_h"], wo, lsem.at[3]))
    loads += [pltpu.make_async_copy(ref["wgu_h"].at[j], wgu.at[:, j * FF : (j + 1) * FF], lsem.at[4 + j]) for j in range(2)]
    loads.append(pltpu.make_async_copy(ref["wd_h"], wd, lsem.at[6]))
    for load in loads:
        load.start()

    barrier = pltpu.get_barrier_semaphore()
    partners = [place.z(d) for d in (1, 2, 3)]
    partners += [place.xs(d) for d in (1, 2, 3)] + [place.ys(d) for d in (1, 2, 3)] + [place.core()]
    for device in partners:
        pl.semaphore_signal(barrier, inc=1, device_id=device, device_id_type=MESH)

    @pl.loop(0, 8)
    def _(r):
        v = tok[sixteen(r), :].astype(F32)
        inv = lax.rsqrt(jnp.mean(v * v, axis=-1, keepdims=True) + EPS)
        attn[own_rows(place, r), :] = (v * inv * gain1[...]).astype(BF)

    pl.semaphore_wait(barrier, len(partners))

    ag1 = Gather(place, attn, zs.at[0], zr.at[0], False)
    agm = Gather(place, masked, zs.at[1], zr.at[1], True)
    ag2 = Gather(place, mlp, zs.at[2], zr.at[2], True)
    ag4 = Gather(place, branch, zs.at[3], zr.at[3], False)
    rs1 = Scatter(place, ref["pa"], ref["relay_a"], ref["recv_a"], zs.at[4], zr.at[4])
    rs3 = Scatter(place, ref["pa"], ref["relay_a"], ref["recv_a"], zs.at[5], zr.at[5])
    rs4 = Scatter(place, ref["pa"], ref["relay_a"], ref["recv_a"], zs.at[6], zr.at[6])
    rs2 = Scatter(place, ref["pb"], ref["relay_b"], ref["recv_b"], zs.at[7], zr.at[7])

    ag1.start()

    cot_load.wait()

    @pl.loop(0, 8)
    def _(r):
        at = place.t * ROWS + r * 16 + lax.broadcasted_iota(jnp.int32, (16, 1), 0)
        v = masked[sixteen(r), :].astype(F32)
        masked[sixteen(r), :] = jnp.where(at < live_rows, v, 0.0).astype(BF)

    def project(slot):
        block = (place.t + OFFS[slot]) % 4
        rows = pl.ds(pl.multiple_of(block * 128, 128), 128)
        for j in range(3):
            p = nn(attn[rows, :], wq[:, j * 512 : (j + 1) * 512])
            if j == 2:
                qkv[rows, 1024:1536] = p.astype(BF)
                continue
            for h in range(HEADS):
                v = p[:, h * HD : (h + 1) * HD]
                v = v * cos_t[rows, :] + pltpu.roll(v, 64, 1) * sin_t[rows, :]
                if j == 0:
                    v = v * HD ** (-0.5)
                qkv[rows, j * 512 + h * HD : j * 512 + (h + 1) * HD] = v.astype(BF)

    for load in loads[:3]:
        load.wait()
    project(0)
    ag1.relay()
    ag1.near()
    agm.start()
    project(1)
    project(2)
    ag1.far()
    project(3)

    @pl.loop(0, HEADS)
    def _(h):
        def cols(j):
            return pl.ds(pl.multiple_of(j * 512 + h * HD, HD), HD)

        for q in range(2):
            rows, keys = pl.ds(q * 256, 256), (q + 1) * 256
            scores = nt(qkv[rows, cols(0)], qkv[0:keys, cols(1)])
            at = q * 256 + lax.broadcasted_iota(jnp.int32, (256, keys), 0)
            key = lax.broadcasted_iota(jnp.int32, (256, keys), 1)
            scores = jnp.where((key <= at) & (key < live_rows), scores, -1e30)
            e = jnp.exp(scores - jnp.max(scores, axis=-1, keepdims=True))
            p = (e * (1.0 / jnp.sum(e, axis=-1, keepdims=True))).astype(BF)
            probs[h, rows, 0:keys] = p
            ctx[rows, cols(0)] = nn(p, qkv[0:keys, cols(2)]).astype(BF)

    loads[3].wait()

    @pl.loop(0, 4)
    def _(n):
        at = pl.ds(pl.multiple_of(n * 512, 512), 512)
        rs1.part[:, at] = nn(in_order(place, ctx, slice(None)), wo[:, at]).astype(BF)
        rs1.start(n, 0, 2, 1, 3)

    other = 1 - place.c
    xs, xr = ref["xs"], ref["xr"]

    def swap_a(group):
        src = (masked, mlp, branch, attn)[group]
        return remote(src, xa.at[group], xs.at[group], xr.at[group], place.core())

    def swap_masked(part):
        rows = (slice(0, 384), slice(384, 512))[part]
        sem = (0, 14)[part]
        return remote(masked.at[rows], xa0.at[rows], xs.at[sem], xr.at[sem], place.core())

    def swap_b(k):
        rows = pl.ds((0, 256, 0, 256, 0, 0)[k], 256 if k < 4 else 512)
        if k < 2:
            src = hid.at[rows, pl.ds(pl.multiple_of(other * 640, 128), 768)]
        elif k < 4:
            src = ggu.at[rows, pl.ds(pl.multiple_of(other * FF, 128), FF)]
        elif k == 4:
            src = ctx.at[rows, pl.ds(pl.multiple_of(other * 256, 256), 256)]
        else:
            src = gproj.at[rows, pl.ds(pl.multiple_of(other * 768, 256), 768)]
        dst = (xb0, xb0, xb1, xb1, xb2, xb0)[k].at[rows]
        return remote(src, dst, xs.at[4 + k], xr.at[4 + k], place.core())

    swap_a(3).start()
    swap_b(4).start()

    rs1.relay(0, 4)
    rs1.finish()

    @pl.loop(0, 8)
    def _(r):
        rows = sixteen(r)
        v = tok[rows, :].astype(F32) + rs1.total(rows)
        middle[rows, :] = v
        inv = lax.rsqrt(jnp.mean(v * v, axis=-1, keepdims=True) + EPS)
        mlp[rows, :] = (v * inv * gain2[...]).astype(BF)

    rs1.done()
    ag2.start()
    for load in loads[4:]:
        load.wait()

    own_b = (
        hid.at[:, pl.ds(pl.multiple_of(place.c * 640, 128), 768)],
        ggu.at[:, pl.ds(pl.multiple_of(place.c * FF, 128), FF)],
        ctx.at[:, pl.ds(pl.multiple_of(place.c * 256, 256), 256)],
        gproj.at[:, pl.ds(pl.multiple_of(place.c * 768, 256), 768)],
    )
    own_a = (masked, mlp, branch, attn)
    other_a = (xa0, ref["pb"], wd.at[0:512], wd.at[512:1024])
    other_b = (xb0, xb1, xb2, xb0)
    osem = ref["osem"]

    def bring(group):
        return pltpu.make_async_copy(xa.at[group], other_a[group], osem.at[group])

    def fetch(group):
        swap_a(group).wait_recv()
        bring(group).start()

    def piece(group, axis, tile, first, count):
        if group == 3 and axis == 1:
            return mlp.at[pl.ds(first, count), pl.ds(pl.multiple_of(tile * 384, 128), 384)]
        base = (FF, 0, FF + 768, FF + 1024)[group]
        lo = base if axis == 0 else base + CX[group]
        width = CX[group] if axis == 0 else CY[group]
        rows = pl.ds(pl.multiple_of(tile * 512 + first, min(count, 128)), count)
        return wgu.at[rows, lo : lo + width]

    p1xs, p1xr, p1ys, p1yr = ref["p1xs"], ref["p1xr"], ref["p1ys"], ref["p1yr"]

    def send_x(group, kind, tile):
        to = 1 - 2 * (tile // 2)
        rows = pl.ds(pl.multiple_of(tile * 128, 128), 128)
        if kind == 0:
            block, dst = place.x + 2, relx[group].at[rows]
        elif kind == 1:
            block, dst, to = place.x + 4 - to, recx[group].at[(1 + to) // 2, rows], -to
        else:
            block, dst = place.x + 4 + to, recx[group].at[(1 - to) // 2, rows]
        src = piece(group, 0, tile, pl.multiple_of((block % 4) * 128, 128), 128)
        sem = (group * 3 + kind) * 4 + tile
        return remote(src, dst, p1xs.at[sem], p1xr.at[sem], place.xs(4 + to))

    def send_y(group, k):
        offset, first, dst, to = (
            (2, 0, rely[group].at[0:256], 1),
            (1, 256, recy[group].at[0, 256:512], 1),
            (2, 256, rely[group].at[256:512], 3),
            (3, 0, recy[group].at[1, 0:256], 3),
            (1, 0, recy[group].at[0, 0:256], 1),
            (3, 256, recy[group].at[1, 256:512], 3),
        )[k]
        src = piece(group, 1, (place.y + offset) % 4, first, 256)
        return remote(src, dst, p1ys.at[group * 6 + k], p1yr.at[group * 6 + k], place.ys(to))

    def gradient(group, step):
        tile = (place.y + jnp.where(step == 0, 2, jnp.where(step == 1, 1, jnp.where(step == 2, 3, 0)))) % 4
        at = pl.ds(pl.multiple_of(tile * 512, 512), 512)
        lo = 0
        for axis, width in ((0, CX[group]), (1, CY[group])):
            own, oth = own_b[group].at[:, lo : lo + width], other_b[group].at[:, lo : lo + width]
            out = tn(own_a[group][:, at], own[...]) + tn(other_a[group][:, at], oth[...])
            piece(group, axis, tile, 0, 512)[...] = out.astype(BF)
            lo += width
        send_x(group, 0, tile).start()
        send_x(group, 1, tile).start()
        for k, when in ((0, 0), (2, 0), (1, 1), (3, 2)):

            @pl.when(step == when)
            def _():
                send_y(group, k).start()

    lands = ref["lands"]

    def mid_copies(group):
        return (
            pltpu.make_async_copy(relx[group], hid.at[:, 0 : CX[group]], lands.at[16 + group]),
            pltpu.make_async_copy(rely[group], hid.at[:, 768 : 768 + CY[group]], lands.at[20 + group]),
        )

    def mid_start(group):
        for tile in range(4):
            send_x(group, 0, tile).wait_recv()
        for k in (0, 2):
            send_y(group, k).wait_recv()
        for copy in mid_copies(group):
            copy.start()

    def mid_end(group):
        for copy in mid_copies(group):
            copy.wait()

        def add(axis, tile, first, rows, lo, width, count):
            @pl.loop(0, count // 32)
            def _(i):
                own = piece(group, axis, tile, pl.multiple_of(first + i * 32, 32), 32)
                got = hid[pl.ds(pl.multiple_of(rows + i * 32, 32), 32), lo : lo + width]
                own[...] = (own[...].astype(F32) + got.astype(F32)).astype(BF)

        for tile in range(4):
            to = 1 if tile < 2 else 3
            add(0, tile, ((place.x + to) % 4) * 128, tile * 128, 0, CX[group], 128)
            send_x(group, 2, tile).start()
        for k, offset, first in ((4, 1, 0), (5, 3, 256)):
            add(1, (place.y + offset) % 4, first, first, 768, CY[group], 256)
            send_y(group, k).start()

    def feed(first, count):
        rows = slice(first, first + count)
        for n0, n1 in ((0, 512), (512, 1024), (1024, 1408)):
            gate = nn(mlp[rows, :], wgu[:, n0:n1])
            up = nn(mlp[rows, :], wgu[:, FF + n0 : FF + n1])
            sig = jax.nn.sigmoid(gate)
            silu = gate * sig
            hid[rows, n0:n1] = (silu * up).astype(BF)
            ggu[rows, n0:n1] = (up * sig * (1.0 + gate * (1.0 - sig))).astype(BF)
            ggu[rows, FF + n0 : FF + n1] = silu.astype(BF)

    def feed_back(first, count, *sends):
        rows = slice(first, first + count)
        for n0, n1 in ((0, 512), (512, 1024), (1024, 1408)):
            grad = nt(masked[rows, :], wd[n0:n1, :])
            for lo in (0, FF):
                ggu[rows, lo + n0 : lo + n1] = (grad * ggu[rows, lo + n0 : lo + n1].astype(F32)).astype(BF)

        @pl.loop(0, 4)
        def _(n):
            at = pl.ds(pl.multiple_of(n * 512, 512), 512)
            rs3.part[rows, at] = nt(ggu[rows, :], wgu[at, :]).astype(BF)
            rs3.start(n, *sends)

    feed(0, 128)
    feed_back(0, 128)
    ag2.relay()
    agm.near()
    agm.relay()
    swap_masked(0).start()
    feed(128, 128)
    feed_back(128, 128, 1, 3)
    swap_b(0).start()
    swap_b(2).start()
    ag2.near()
    ag2.far()
    swap_a(1).start()
    feed(256, 256)
    swap_b(1).start()
    agm.far()
    swap_masked(1).start()
    feed_back(256, 256, 0, 2)
    swap_b(3).start()
    fetch(1)

    p2xs, p2xr, p2ys, p2yr = ref["p2xs"], ref["p2xr"], ref["p2ys"], ref["p2yr"]

    def landing(group):
        copies = []
        for d in range(2):
            for axis, src in ((0, recx[group]), (1, recy[group])):
                lo = d * FF + axis * 768
                width = CX[group] if axis == 0 else CY[group]
                sem = lands.at[group * 4 + d * 2 + axis]
                copies.append(pltpu.make_async_copy(src.at[d], ggu.at[:, lo : lo + width], sem))
        return copies

    def send_2(group, axis, d):
        sem = group * 3 + d - 1
        own = pl.multiple_of(place.x * 128, 128)
        if axis == 0:
            src = piece(group, 0, (place.y + d) % 4, own, 128)
            dst = r2.at[d - 1, :, BASE[group] : BASE[group] + CX[group]]
            return remote(src, dst, p2xs.at[sem], p2xr.at[sem], place.ys(d))
        src = piece(group, 1, place.y, pl.multiple_of(((place.x + d) % 4) * 128, 128), 128)
        dst = r2.at[d - 1, :, BASE[group] + CX[group] : BASE[group] + COLS[group]]
        return remote(src, dst, p2ys.at[sem], p2yr.at[sem], place.xs(d))

    def land(group):
        for tile in range(4):
            for kind in (1, 2):
                send_x(group, kind, tile).wait_recv()
        for k in (1, 3, 4, 5):
            send_y(group, k).wait_recv()
        for copy in landing(group):
            copy.start()

    def first_sum(group):
        for copy in landing(group):
            copy.wait()
        for axis in range(2):
            lo = axis * 768
            width = CX[group] if axis == 0 else CY[group]

            @pl.loop(0, 16)
            def _(i):
                if axis == 0:
                    own = piece(group, 0, i // 4, pl.multiple_of(place.x * 128 + (i % 4) * 32, 32), 32)
                else:
                    own = piece(group, 1, place.y, pl.multiple_of(i * 32, 32), 32)
                rows = pl.ds(pl.multiple_of(i * 32, 32), 32)
                total = own[...].astype(F32)
                for d in range(2):
                    total = total + ggu[rows, d * FF + lo : d * FF + lo + width].astype(F32)
                own[...] = total.astype(BF)

            for d in (2, 1, 3):
                send_2(group, axis, d).start()

    def whole_of(group):
        return ((final, 0), (middle, 0), (final, 768), (final, 1024))[group]

    def ending(group):
        ref_at, first = whole_of(group)
        cols = slice(first, first + COLS[group])
        mine = ref_at.at[pl.ds(pl.multiple_of(place.c * 64, 64), 64), cols]
        theirs = ref_at.at[pl.ds(pl.multiple_of(other * 64, 64), 64), cols]
        dst = shares.at[place.c, :, BASE[group] : BASE[group] + COLS[group]]
        return (
            remote(theirs, dst, xs.at[10 + group], xr.at[10 + group], place.core()),
            pltpu.make_async_copy(mine, dst, lsem.at[9 + group]),
        )

    def second_sum(group):
        for axis in range(2):
            for d in (1, 2, 3):
                send_2(group, axis, d).wait_recv()
            lo = BASE[group] + (0 if axis == 0 else CX[group])
            width = CX[group] if axis == 0 else CY[group]
            whole, first = whole_of(group)
            first += lo - BASE[group]

            @pl.loop(0, 4)
            def _(i):
                rows = pl.ds(pl.multiple_of(i * 32, 32), 32)
                own = piece(group, axis, place.y, pl.multiple_of(place.x * 128 + i * 32, 32), 32)
                total = own[...].astype(F32)
                for d in range(3):
                    total = total + r2[d, rows, lo : lo + width].astype(F32)
                whole[rows, first : first + width] = total
        for copy in ending(group):
            copy.start()

    swap_b(0).wait_recv()
    swap_b(1).wait_recv()
    swap_masked(0).wait_recv()
    swap_masked(1).wait_recv()

    @pl.loop(0, 2)
    def _(step):
        gradient(0, step)

    rs3.relay(0, 2)

    @pl.loop(2, 4)
    def _(step):
        gradient(0, step)

    rs3.relay(2, 4)
    bring(1).wait()
    swap_b(2).wait_recv()
    swap_b(3).wait_recv()

    @pl.loop(0, 2)
    def _(step):
        gradient(1, step)

    rs3.finish()

    def fold(v):
        return jnp.concatenate([v[:, i * 512 : (i + 1) * 512] for i in range(4)], axis=0)

    def mlp_back(r, total):
        rows = sixteen(r)
        grad = rs3.total(rows)
        v = middle[rows, :]
        inv = lax.rsqrt(jnp.mean(v * v, axis=-1, keepdims=True) + EPS)
        scaled = grad * gain2[...]
        back = (
            masked[rows, :].astype(F32)
            + inv * scaled
            - v * (inv * inv * inv) * jnp.mean(v * scaled, axis=-1, keepdims=True)
        )
        gmid[rows, :] = back
        branch[own_rows(place, r), :] = back.astype(BF)
        return total + jnp.sum(grad * v * inv, axis=0, keepdims=True)

    gain2_part = lax.fori_loop(0, 8, mlp_back, jnp.zeros((1, D), F32))
    gacc[0, 4:8, :] = fold(gain2_part)
    ag4.start()
    rs3.done()

    @pl.loop(2, 4)
    def _(step):
        gradient(1, step)

    @pl.loop(0, 4)
    def _(n):
        at = pl.ds(pl.multiple_of(n * 512, 512), 512)
        rs2.part[:, at] = nn(hid[...], wd[:, at]).astype(BF)

    fetch(3)
    for k in (0, 1, 2, 3):
        swap_b(k).wait_send()
    mid_start(0)
    ag4.relay()

    @pl.loop(0, 4)
    def _(n):
        rs2.start(n, 0, 2, 1, 3)

    mid_end(0)
    mid_start(1)
    mid_end(1)
    ag4.near()
    ag4.far()
    swap_a(2).start()

    @pl.loop(0, 2)
    def _(n):
        at = pl.ds(pl.multiple_of(n * 256, 256), 256)
        gctx[:, at] = nt(branch[...], wo[at, :]).astype(BF)


    def turn_back(v, rows):
        return v * cos_t[rows, :] - pltpu.roll(v, 64, 1) * sin_t[rows, :]

    @pl.loop(0, HEADS)
    def _(h):
        def cols(j):
            return pl.ds(pl.multiple_of(j * 512 + h * HD, HD), HD)

        def part(q):
            rows, keys = pl.ds(q * 256, 256), (q + 1) * 256
            p = probs[h, rows, 0:keys]
            grad = gctx[rows, cols(0)]
            wide = p.astype(F32)
            gp = nt(grad, qkv[0:keys, cols(2)])
            gs = (wide * (gp - jnp.sum(wide * gp, axis=-1, keepdims=True))).astype(BF)
            gq = (turn_back(nn(gs, qkv[0:keys, cols(1)]), rows) * HD ** (-0.5)).astype(BF)
            return gq, tn(gs, qkv[rows, cols(0)]), tn(p, grad)

        q1, k1, v1 = part(1)
        q0, k0, v0 = part(0)
        lo, hi = slice(0, 256), slice(256, 512)
        k0, k1 = turn_back(k0 + k1[lo], lo).astype(BF), turn_back(k1[hi], hi).astype(BF)
        v0, v1 = (v0 + v1[lo]).astype(BF), v1[hi].astype(BF)
        for j, low, high in ((0, q0, q1), (1, k0, k1), (2, v0, v1)):
            gproj[lo, cols(j)] = low
            gproj[hi, cols(j)] = high

    fetch(2)
    swap_b(5).start()

    def attn_part(n):
        at = pl.ds(pl.multiple_of(n * 512, 512), 512)
        part = nt(in_order(place, gproj, slice(None)), wq[at, :])
        rs4.part[:, at] = part.astype(BF)
        rs4.start(n, 0, 2, 1, 3)
        seen = jnp.sum(part * in_order(place, attn, at).astype(F32), axis=0, keepdims=True)
        gsum[n] = jnp.broadcast_to(seen, (8, 512))

    @pl.loop(0, 2)
    def _(n):
        attn_part(n)

    rs2.relay(0, 4)
    land(0)
    first_sum(0)
    swap_a(1).wait_send()
    ag2.done()
    bring(3).wait()
    swap_b(5).wait_recv()

    @pl.loop(0, 4)
    def _(step):
        gradient(3, step)

    @pl.loop(2, 4)
    def _(n):
        attn_part(n)

    for n in range(4):
        at = slice(n * 512, (n + 1) * 512)
        gacc[0, n : n + 1, :] = gsum[n, 0:1, :] / gain1[:, at]
    gs, gr = ref["gs"], ref["gr"]

    def spread(stage):
        count = 2 if stage == 3 else 4
        me = (place.t, place.x, place.y, place.c)[stage]
        out = []
        for d in range(1, count):
            device = (place.z, place.xs, place.ys, lambda _: place.core())[stage](d)
            k = stage * 3 + d - 1
            out.append(remote(gacc.at[stage], grecv.at[stage * 4 + me], gs.at[k], gr.at[k], device))
        return out, count, me

    def spread_start(stage):
        copies, _, me = spread(stage)
        grecv[stage * 4 + me] = gacc[stage]
        for copy in copies:
            copy.start()

    def spread_end(stage):
        copies, count, _ = spread(stage)
        for copy in copies:
            copy.wait_recv()
        total = grecv[stage * 4]
        for i in range(1, count):
            total = total + grecv[stage * 4 + i]
        gacc[stage + 1] = total

    spread_start(0)
    swap_b(4).wait_recv()
    bring(2).wait()

    @pl.loop(0, 4)
    def _(step):
        gradient(2, step)

    land(1)
    first_sum(1)
    rs4.relay(0, 4)
    rs2.finish()

    @pl.loop(0, 8)
    def _(r):
        rows = sixteen(r)
        middle[rows, :] = middle[rows, :] + rs2.total(rows)

    out_copy = pltpu.make_async_copy(middle, ref["output"], lsem.at[7])
    out_copy.start()
    mid_start(3)
    spread_end(0)
    spread_start(1)
    mid_end(3)
    mid_start(2)
    second_sum(0)
    mid_end(2)
    spread_end(1)
    spread_start(2)
    land(3)
    first_sum(3)
    land(2)
    first_sum(2)
    out_copy.wait()
    second_sum(1)
    spread_end(2)
    spread_start(3)
    rs4.finish()

    @pl.loop(0, 8)
    def _(r):
        rows = sixteen(r)
        grad = rs4.total(rows)
        v = tok[rows, :].astype(F32)
        inv = lax.rsqrt(jnp.mean(v * v, axis=-1, keepdims=True) + EPS)
        scaled = grad * gain1[...]
        gmid[rows, :] = (
            gmid[rows, :]
            + inv * scaled
            - v * (inv * inv * inv) * jnp.mean(v * scaled, axis=-1, keepdims=True)
        )

    tok_copy = pltpu.make_async_copy(gmid, ref["grad_tokens"], lsem.at[8])
    tok_copy.start()
    second_sum(3)
    second_sum(2)
    spread_end(3)
    ref["gains"][...] = gacc[4]

    for gather in (ag1, agm, ag4):
        gather.done()
    rs4.done()
    rs2.done()
    for group in (2, 3):
        swap_a(group).wait_send()
    swap_masked(0).wait_send()
    swap_masked(1).wait_send()
    for k in (4, 5):
        swap_b(k).wait_send()
    for group in range(4):
        for tile in range(4):
            for kind in range(3):
                send_x(group, kind, tile).wait_send()
        for k in range(6):
            send_y(group, k).wait_send()
        for d in (1, 2, 3):
            for axis in range(2):
                send_2(group, axis, d).wait_send()
    for stage in range(4):
        for copy in spread(stage)[0]:
            copy.wait_send()
    tok_copy.wait()
    for group in range(4):
        for copy in ending(group):
            copy.wait()


def block(tokens, gain_attn, w_qkv, w_out, gain_mlp, w_gate_up, w_down, cotangent, lengths):
    cos_t, sin_t = rotary_tables()
    vmem = pl.BlockSpec(memory_space=pltpu.VMEM)
    smem = pl.BlockSpec(memory_space=pltpu.SMEM)
    hbm = pl.BlockSpec(memory_space=pl.ANY)
    ins = [
        ("tok", tokens, vmem),
        ("gain1", gain_attn.reshape(1, D), vmem),
        ("wq_h", w_qkv, hbm),
        ("wo_h", w_out, hbm),
        ("gain2", gain_mlp.reshape(1, D), vmem),
        ("wgu_h", w_gate_up, hbm),
        ("wd_h", w_down, hbm),
        ("cot", cotangent, hbm),
        ("lengths", lengths, smem),
        ("cos", jnp.asarray(cos_t), vmem),
        ("sin", jnp.asarray(sin_t), vmem),
    ]
    outs = [
        ("output", (ROWS, D), F32, hbm),
        ("grad_tokens", (ROWS, D), F32, hbm),
        ("gains", (8, 512), F32, vmem),
        ("shares", (2, 64, ALL), F32, hbm),
        ("xa", (4, SEQ, D), BF, hbm),
    ]
    outs += [(f"relx{g}", (SEQ, CX[g]), BF, hbm) for g in range(4)]
    outs += [(f"rely{g}", (SEQ, CY[g]), BF, hbm) for g in range(4)]
    outs += [(f"recx{g}", (2, SEQ, CX[g]), BF, hbm) for g in range(4)]
    outs += [(f"recy{g}", (2, SEQ, CY[g]), BF, hbm) for g in range(4)]
    dma = pltpu.SemaphoreType.DMA
    scratch = [
        ("wq", pltpu.VMEM((D, 1536), BF)),
        ("wo", pltpu.VMEM((512, D), BF)),
        ("wgu", pltpu.VMEM((D, 2 * FF), BF)),
        ("wd", pltpu.VMEM((FF, D), BF)),
        ("attn", pltpu.VMEM((SEQ, D), BF)),
        ("qkv", pltpu.VMEM((SEQ, 1536), BF)),
        ("probs", pltpu.VMEM((HEADS, SEQ, SEQ), BF)),
        ("ctx", pltpu.VMEM((SEQ, 512), BF)),
        ("middle", pltpu.VMEM((ROWS, D), F32)),
        ("mlp", pltpu.VMEM((SEQ, D), BF)),
        ("masked", pltpu.VMEM((SEQ, D), BF)),
        ("branch", pltpu.VMEM((SEQ, D), BF)),
        ("hid", pltpu.VMEM((SEQ, FF), BF)),
        ("ggu", pltpu.VMEM((SEQ, 2 * FF), BF)),
        ("gctx", pltpu.VMEM((SEQ, 512), BF)),
        ("xa0", pltpu.VMEM((SEQ, D), BF)),
        ("xb0", pltpu.VMEM((SEQ, COLS[0]), BF)),
        ("xb1", pltpu.VMEM((SEQ, COLS[1]), BF)),
        ("xb2", pltpu.VMEM((SEQ, COLS[2]), BF)),
        ("gmid", pltpu.VMEM((ROWS, D), F32)),
        ("pa", pltpu.VMEM((SEQ, D), BF)),
        ("relay_a", pltpu.VMEM((2, 64, D), BF)),
        ("recv_a", pltpu.VMEM((2, ROWS, D), BF)),
        ("pb", pltpu.VMEM((SEQ, D), BF)),
        ("relay_b", pltpu.VMEM((2, 64, D), BF)),
        ("recv_b", pltpu.VMEM((2, ROWS, D), BF)),
        ("r2", pltpu.VMEM((3, ROWS, ALL), BF)),
        ("final", pltpu.VMEM((ROWS, 1792), F32)),
        ("gacc", pltpu.VMEM((5, 8, 512), F32)),
        ("gsum", pltpu.VMEM((4, 8, 512), F32)),
        ("grecv", pltpu.VMEM((14, 8, 512), F32)),
        ("zs", dma((8, 24))),
        ("zr", dma((8, 24))),
        ("lsem", dma((13,))),
        ("osem", dma((4,))),
        ("xs", dma((15,))),
        ("xr", dma((15,))),
        ("p1xs", dma((48,))),
        ("p1xr", dma((48,))),
        ("p1ys", dma((24,))),
        ("p1yr", dma((24,))),
        ("p2xs", dma((12,))),
        ("p2xr", dma((12,))),
        ("p2ys", dma((12,))),
        ("p2yr", dma((12,))),
        ("lands", dma((24,))),
        ("gs", dma((10,))),
        ("gr", dma((10,))),
    ]
    names = [i[0] for i in ins] + [o[0] for o in outs] + [s[0] for s in scratch]
    results = pl.pallas_call(
        functools.partial(kernel, names),
        out_shape=[jax.ShapeDtypeStruct(o[1], o[2]) for o in outs],
        in_specs=[i[2] for i in ins],
        out_specs=[o[3] for o in outs],
        scratch_shapes=[s[1] for s in scratch],
        compiler_params=pltpu.CompilerParams(
            collective_id=0, has_side_effects=True, vmem_limit_bytes=63 * 1024 * 1024
        ),
        name="block",
    )(*[i[1] for i in ins])
    return arrange(*results[:4])


def arrange_kernel(out_in, tok_in, gains, shares, output, grad_tokens, gain1, qkv, out, gain2, gate_up, down, *scratch):
    out_v, tok_v, shares_v, sem = scratch
    down_at, gu_at, out_at, qkv_at = BASE
    loads = [
        pltpu.make_async_copy(src, dst, sem.at[i])
        for i, (src, dst) in enumerate(((out_in, out_v), (tok_in, tok_v), (shares, shares_v)))
    ]
    for load in loads:
        load.start()

    def columns(core, first, count):
        return shares_v.at[core, :, first : first + count]

    moves = (
        ((out_v, output),),
        ((tok_v, grad_tokens),),
        (
            (columns(0, gu_at, FF), gate_up.at[0]),
            (columns(1, gu_at, FF), gate_up.at[1]),
            (columns(0, qkv_at, 512), qkv.at[0]),
            (columns(0, qkv_at + 512, 256), qkv.at[1, :, 0:256]),
            (columns(1, qkv_at, 256), qkv.at[1, :, 256:512]),
            (columns(1, qkv_at + 256, 512), qkv.at[2]),
            (columns(0, down_at, 768), down.at[:, 0:768]),
            (columns(1, down_at + 128, 640), down.at[:, 768:1408]),
            (columns(0, out_at, 256), out.at[:, 0:256]),
            (columns(1, out_at, 256), out.at[:, 256:512]),
        ),
    )
    for i in range(4):
        at = slice(i * 512, (i + 1) * 512)
        gain1[:, at] = gains[i : i + 1, :]
        gain2[:, at] = gains[4 + i : 5 + i, :]
    stores = []
    for load, group in zip(loads, moves):
        load.wait()
        for src, dst in group:
            stores.append(pltpu.make_async_copy(src, dst, sem.at[3 + len(stores)]))
            stores[-1].start()
    for store in stores:
        store.wait()


def arrange(output, grad_tokens, gains, shares):
    vmem = pl.BlockSpec(memory_space=pltpu.VMEM)
    hbm = pl.BlockSpec(memory_space=pl.ANY)
    outs = (
        ((ROWS, D), hbm),
        ((ROWS, D), hbm),
        ((1, D), vmem),
        ((3, 64, 512), hbm),
        ((64, 512), hbm),
        ((1, D), vmem),
        ((2, 64, FF), hbm),
        ((64, FF), hbm),
    )
    results = pl.pallas_call(
        arrange_kernel,
        out_shape=[jax.ShapeDtypeStruct(o[0], F32) for o in outs],
        in_specs=[hbm, hbm, vmem, hbm],
        out_specs=[o[1] for o in outs],
        scratch_shapes=[
            pltpu.VMEM((ROWS, D), F32),
            pltpu.VMEM((ROWS, D), F32),
            pltpu.VMEM((2, 64, ALL), F32),
            pltpu.SemaphoreType.DMA((15,)),
        ],
        compiler_params=pltpu.CompilerParams(vmem_limit_bytes=63 * 1024 * 1024),
        name="arrange",
    )(output, grad_tokens, gains, shares)
    output, grad_tokens, gain1, qkv, out, gain2, gate_up, down = results
    return output, grad_tokens, gain1.reshape(D), qkv, out.T, gain2.reshape(D), gate_up, down.T


def solution(mesh):
    placed = (
        P(("dp", "tensor"), None),
        P(),
        P(None, None, "tensor"),
        P("tensor", None),
        P(),
        P(None, None, "tensor"),
        P("tensor", None),
        P(("dp", "tensor"), None),
        P("dp"),
    )
    return jax.shard_map(
        block,
        mesh=mesh,
        in_specs=placed,
        out_specs=(
            P(("dp", "tensor"), None),
            P(("dp", "tensor"), None),
            P(),
            P(None, "dp", "tensor"),
            P("tensor", "dp"),
            P(),
            P(None, "dp", "tensor"),
            P("tensor", "dp"),
        ),
        check_vma=False,
    )
```

time: 224 us -> 182 us (0.81)
  Pallas kernels: 211 us -> 181 us
  local copies, waits for them, and re-layouts: 10.1 us -> 0 us
    pallas_call x1, Pallas kernels: 211 us -> 176 us  [block(): pl.pallas_call(functools.partial(kernel, names), out_shape=[jax.ShapeDtyp...]
    unnamed x10 -> x0, local copies, waits for them, and re-layouts: 4.82 us -> none
    pallas_call x0 -> x1, Pallas kernels: none -> 4.66 us  [arrange(): pl.pallas_call(arrange_kernel, out_shape=[jax.ShapeDtypeStruct(o[0], F32)...]
    squeeze x3 -> x0, local copies, waits for them, and re-layouts: 2.96 us -> none  [the longest x2 2.08 us: block(): down = jnp.concatenate([shares[0, :, 0:768], shares[1, :, 128:768]], axis=1)]
where the time goes in v2:
time: 182 us
  Pallas kernels  181 us (99%)
    pallas_call x1, Pallas kernels, block(): pl.pallas_call(functools.partial(kernel, names), out_shape=[jax.ShapeDtyp...  176 us
    pallas_call x1, Pallas kernels, arrange(): pl.pallas_call(arrange_kernel, out_shape=[jax.ShapeDtypeStruct(o[0], F32)...  4.66 us

profile of v2, /device:TPU:1, one launch (start us, length us, event | category | flops | bytes accessed | tf_op | source)
XLA Modules:
  0.0 182.0 jit_solution(955837853269443483)
XLA Ops:
  1.3 175.9 %block.1 = (f32[128,2048]{1,0:T(8,128)}, f32[128,2048]{1,0:T(8,128)}, f32[8,512]{1,0:T(8,128)}, f32[2,64,3200]{2,1,0:T(8,128)}, bf16[4,512,2048]{2,1,0:T(8,128)(...) custom-call(bf16[128,2048]{1,0:T(8,128)(2,1)} %refs_0_.1, ...), custom_call_target="tpu_custom_call" | custom-call | tf_op jit(solution)/shard_map/block/pallas_call | solution.py:932
  177.2 4.7 %arrange.1 = (f32[128,2048]{1,0:T(8,128)}, f32[128,2048]{1,0:T(8,128)}, f32[1,2048]{1,0:T(1,128)}, f32[3,64,512]{2,1,0:T(8,128)}, f32[64,512]{1,0:T(8,128)}, /*i...) custom-call(f32[128,2048]{1,0:T(8,128)} %get-tuple-element.20.out_in, ...), custom_call_target="tpu_custom_call" | custom-call | tf_op jit(solution)/shard_map/arrange/pallas_call | solution.py:1002

commit v3 on v2

--- a/solution.py
+++ b/solution.py
@@ -111,8 +111,8 @@
         dst = self.buf.at[self.row(there, half)] if self.relative else src
         return remote(src, dst, self.ssem.at[k], self.rsem.at[k], self.place.z(to))
 
-    def start(self):
-        for k in (0, 2, 1, 3):
+    def start(self, *which):
+        for k in which or (0, 2, 1, 3):
             self.copy(k).start()
 
     def relay(self):
@@ -205,12 +205,11 @@
     tok, cot, live = ref["tok"], ref["cot"], ref["lengths"]
     wq, wo, wgu, wd = ref["wq"], ref["wo"], ref["wgu"], ref["wd"]
     attn, qkv, probs, ctx = ref["attn"], ref["qkv"], ref["probs"], ref["ctx"]
-    middle, mlp, masked, branch = ref["middle"], ref["mlp"], ref["masked"], ref["branch"]
+    middle, mlp, masked, w3 = ref["middle"], ref["mlp"], ref["masked"], ref["w3"]
+    pa, pb, branch = w3.at[0], w3.at[1], w3.at[2]
     hid, ggu, gctx, gproj, gmid = ref["hid"], ref["ggu"], ref["gctx"], ref["qkv"], ref["gmid"]
     cos_t, sin_t, gain1, gain2 = ref["cos"], ref["sin"], ref["gain1"], ref["gain2"]
     xa, xa0, xb0, xb1, xb2 = ref["xa"], ref["xa0"], ref["xb0"], ref["xb1"], ref["xb2"]
-    relx, rely = [ref[f"relx{g}"] for g in range(4)], [ref[f"rely{g}"] for g in range(4)]
-    recx, recy = [ref[f"recx{g}"] for g in range(4)], [ref[f"recy{g}"] for g in range(4)]
     r2, final, shares = ref["r2"], ref["final"], ref["shares"]
     gacc, grecv, gsum = ref["gacc"], ref["grecv"], ref["gsum"]
     zs, zr, lsem = ref["zs"], ref["zr"], ref["lsem"]
@@ -220,10 +219,12 @@
     cot_load.start()
 
     loads = [pltpu.make_async_copy(ref["wq_h"].at[j], wq.at[:, j * 512 : (j + 1) * 512], lsem.at[j]) for j in range(3)]
+    tables = [pltpu.make_async_copy(ref["cos_h"], cos_t, lsem.at[8])]
+    tables.append(pltpu.make_async_copy(ref["sin_h"], sin_t, lsem.at[9]))
     loads.append(pltpu.make_async_copy(ref["wo_h"], wo, lsem.at[3]))
     loads += [pltpu.make_async_copy(ref["wgu_h"].at[j], wgu.at[:, j * FF : (j + 1) * FF], lsem.at[4 + j]) for j in range(2)]
     loads.append(pltpu.make_async_copy(ref["wd_h"], wd, lsem.at[6]))
-    for load in loads:
+    for load in tables + loads:
         load.start()
 
     barrier = pltpu.get_barrier_semaphore()
@@ -244,13 +245,39 @@
     agm = Gather(place, masked, zs.at[1], zr.at[1], True)
     ag2 = Gather(place, mlp, zs.at[2], zr.at[2], True)
     ag4 = Gather(place, branch, zs.at[3], zr.at[3], False)
-    rs1 = Scatter(place, ref["pa"], ref["relay_a"], ref["recv_a"], zs.at[4], zr.at[4])
-    rs3 = Scatter(place, ref["pa"], ref["relay_a"], ref["recv_a"], zs.at[5], zr.at[5])
-    rs4 = Scatter(place, ref["pa"], ref["relay_a"], ref["recv_a"], zs.at[6], zr.at[6])
-    rs2 = Scatter(place, ref["pb"], ref["relay_b"], ref["recv_b"], zs.at[7], zr.at[7])
-
+    rs3 = Scatter(place, pa, ref["relay_a"], ref["recv_a"], zs.at[5], zr.at[5])
+    rs4 = Scatter(place, pa, ref["relay_a"], ref["recv_a"], zs.at[6], zr.at[6])
+    rs2 = Scatter(place, pb, ref["relay_b"], ref["recv_b"], zs.at[7], zr.at[7])
+
+    ws, wr = ref["ws"], ref["wr"]
+    halves = (slice(0, 1024), slice(1024, 2048))
+    minor, major = (place.x, place.y), (place.y, place.x)
+
+    def w_rows(half, at, count):
+        first = (at * 2 + place.c) * 64
+        if count == 16:
+            first = first + minor[half] * 16
+        return pl.ds(pl.multiple_of(first, 16), count)
+
+    def w_first(half, d):
+        rows, k = w_rows(half, major[half], 16), half * 3 + d - 1
+        dst = w3.at[d - 1, rows, halves[half]]
+        return remote(ref["wo_h"].at[rows, halves[half]], dst, ws.at[k], wr.at[k], place.z(d))
+
+    def w_plane(half, phase, d):
+        part = w3.at[:, w_rows(half, major[half], (16, 64)[phase]), halves[half]]
+        k = 6 + (phase * 2 + half) * 3 + d - 1
+        device = (place.xs, place.ys)[half ^ phase](d)
+        return remote(part, part, ws.at[k], wr.at[k], device)
+
+    def w_core(half, d):
+        part = w3.at[:, w_rows(half, (major[half] + d) % 4, 64), halves[half]]
+        return remote(part, part, ws.at[18 + half * 4 + d], wr.at[18 + half * 4 + d], place.core())
+
+    both = [(half, d) for half in range(2) for d in (1, 2, 3)]
+    for half, d in both:
+        w_first(half, d).start()
     ag1.start()
-
     cot_load.wait()
 
     @pl.loop(0, 8)
@@ -274,12 +301,22 @@
                     v = v * HD ** (-0.5)
                 qkv[rows, j * 512 + h * HD : j * 512 + (h + 1) * HD] = v.astype(BF)
 
-    for load in loads[:3]:
+    for load in tables + loads[:3]:
         load.wait()
     project(0)
+    for half, d in both:
+        w_first(half, d).wait_recv()
+    for half, d in both:
+        w_plane(half, 0, d).start()
     ag1.relay()
+    for half, d in both:
+        w_plane(half, 0, d).wait_recv()
+    for half, d in both:
+        w_plane(half, 1, d).start()
+    for half in range(2):
+        w_core(half, 0).start()
     ag1.near()
-    agm.start()
+    agm.start(0, 2)
     project(1)
     project(2)
     ag1.far()
@@ -301,13 +338,22 @@
             probs[h, rows, 0:keys] = p
             ctx[rows, cols(0)] = nn(p, qkv[0:keys, cols(2)]).astype(BF)
 
+    heads = ref["recv_a"].at[0]
+
+    def to_rows(d):
+        src = ctx.at[pl.ds(pl.multiple_of(((place.t + d) % 4) * 128, 128), 128)]
+        dst = heads.at[:, pl.ds(pl.multiple_of(place.t * 512, 512), 512)]
+        return remote(src, dst, zs.at[4, d - 1], zr.at[4, d - 1], place.z(d))
+
+    for d in (1, 3, 2):
+        to_rows(d).start()
+    agm.start(1, 3)
+    own = pl.ds(pl.multiple_of(place.t * 128, 128), 128)
+    heads[:, pl.ds(pl.multiple_of(place.t * 512, 512), 512)] = ctx[own, :]
+    for half, d in both:
+        w_plane(half, 1, d).wait_recv()
+        w_core(half, (4 - d) % 4).start()
     loads[3].wait()
-
-    @pl.loop(0, 4)
-    def _(n):
-        at = pl.ds(pl.multiple_of(n * 512, 512), 512)
-        rs1.part[:, at] = nn(in_order(place, ctx, slice(None)), wo[:, at]).astype(BF)
-        rs1.start(n, 0, 2, 1, 3)
 
     other = 1 - place.c
     xs, xr = ref["xs"], ref["xr"]
@@ -315,6 +361,12 @@
     def swap_a(group):
         src = (masked, mlp, branch, attn)[group]
         return remote(src, xa.at[group], xs.at[group], xr.at[group], place.core())
+
+    def swap_branch(slot):
+        block = (place.t + OFFS[slot]) % 4
+        rows = pl.ds(pl.multiple_of(block * 128, 128), 128)
+        sem = (2, 15, 16, 17)[slot]
+        return remote(branch.at[rows], xa.at[2, rows], xs.at[sem], xr.at[sem], place.core())
 
     def swap_masked(part):
         rows = (slice(0, 384), slice(384, 512))[part]
@@ -337,18 +389,38 @@
     swap_a(3).start()
     swap_b(4).start()
 
-    rs1.relay(0, 4)
-    rs1.finish()
+    for half in range(2):
+        for d in range(4):
+            w_core(half, d).wait_recv()
+    for d in (1, 2, 3):
+        to_rows(d).wait_recv()
+
+    @pl.loop(0, 4)
+    def _(n):
+        at = pl.ds(pl.multiple_of(n * 512, 512), 512)
+
+        def share(d, weights):
+            return nn(heads[:, pl.ds(pl.multiple_of(((place.t + d) % 4) * 512, 512), 512)], weights)
+
+        out = share(0, wo[:, at]) + share(3, w3[0, :, at]) + share(2, w3[1, :, at]) + share(1, w3[2, :, at])
+        middle[:, at] = tok[:, at].astype(F32) + out
 
     @pl.loop(0, 8)
     def _(r):
         rows = sixteen(r)
-        v = tok[rows, :].astype(F32) + rs1.total(rows)
-        middle[rows, :] = v
+        v = middle[rows, :]
         inv = lax.rsqrt(jnp.mean(v * v, axis=-1, keepdims=True) + EPS)
         mlp[rows, :] = (v * inv * gain2[...]).astype(BF)
 
-    rs1.done()
+    for d in (1, 2, 3):
+        to_rows(d).wait_send()
+    for half, d in both:
+        w_first(half, d).wait_send()
+        w_plane(half, 0, d).wait_send()
+        w_plane(half, 1, d).wait_send()
+    for half in range(2):
+        for d in range(4):
+            w_core(half, d).wait_send()
     ag2.start()
     for load in loads[4:]:
         load.wait()
@@ -360,7 +432,7 @@
         gproj.at[:, pl.ds(pl.multiple_of(place.c * 768, 256), 768)],
     )
     own_a = (masked, mlp, branch, attn)
-    other_a = (xa0, ref["pb"], wd.at[0:512], wd.at[512:1024])
+    other_a = (xa0, pb, wd.at[0:512], wd.at[512:1024])
     other_b = (xb0, xb1, xb2, xb0)
     osem = ref["osem"]
 
@@ -368,7 +440,11 @@
         return pltpu.make_async_copy(xa.at[group], other_a[group], osem.at[group])
 
     def fetch(group):
-        swap_a(group).wait_recv()
+        if group == 2:
+            for slot in range(4):
+                swap_branch(slot).wait_recv()
+        else:
+            swap_a(group).wait_recv()
         bring(group).start()
 
     def piece(group, axis, tile, first, count):
@@ -382,33 +458,49 @@
 
     p1xs, p1xr, p1ys, p1yr = ref["p1xs"], ref["p1xr"], ref["p1ys"], ref["p1yr"]
 
-    def send_x(group, kind, tile):
-        to = 1 - 2 * (tile // 2)
+    def relayed(group, axis):
+        if group < 2:
+            return ref[("relx", "rely")[axis] + str(group)]
+        lo = ((768, 896), (0, 384))[group - 2][axis]
+        return xb1.at[:, lo : lo + CX[group]]
+
+    def arrived(group, axis, side):
+        if group < 2:
+            return ref[("recx", "recy")[axis] + str(group)].at[side]
+        width = CX[group]
+        lo = ((1536, 1792), (0, 768))[group - 2][axis] + side * width
+        return xa0.at[:, pl.ds(lo if isinstance(lo, int) else pl.multiple_of(lo, 128), width)]
+
+    def tile_of(step):
+        return (place.y + jnp.where(step == 0, 2, jnp.where(step == 1, 1, jnp.where(step == 2, 3, 0)))) % 4
+
+    def send_x(group, kind, step):
+        tile, to = tile_of(step), 1 - 2 * (step % 2)
         rows = pl.ds(pl.multiple_of(tile * 128, 128), 128)
         if kind == 0:
-            block, dst = place.x + 2, relx[group].at[rows]
+            block, dst = place.x + 2, relayed(group, 0).at[rows]
         elif kind == 1:
-            block, dst, to = place.x + 4 - to, recx[group].at[(1 + to) // 2, rows], -to
+            block, dst, to = place.x + 4 - to, arrived(group, 0, (1 + to) // 2).at[rows], -to
         else:
-            block, dst = place.x + 4 + to, recx[group].at[(1 - to) // 2, rows]
+            block, dst = place.x + 4 + to, arrived(group, 0, (1 - to) // 2).at[rows]
         src = piece(group, 0, tile, pl.multiple_of((block % 4) * 128, 128), 128)
-        sem = (group * 3 + kind) * 4 + tile
+        sem = (group * 3 + kind) * 4 + step
         return remote(src, dst, p1xs.at[sem], p1xr.at[sem], place.xs(4 + to))
 
     def send_y(group, k):
         offset, first, dst, to = (
-            (2, 0, rely[group].at[0:256], 1),
-            (1, 256, recy[group].at[0, 256:512], 1),
-            (2, 256, rely[group].at[256:512], 3),
-            (3, 0, recy[group].at[1, 0:256], 3),
-            (1, 0, recy[group].at[0, 0:256], 1),
-            (3, 256, recy[group].at[1, 256:512], 3),
+            (2, 0, relayed(group, 1).at[0:256], 1),
+            (1, 256, arrived(group, 1, 0).at[256:512], 1),
+            (2, 256, relayed(group, 1).at[256:512], 3),
+            (3, 0, arrived(group, 1, 1).at[0:256], 3),
+            (1, 0, arrived(group, 1, 0).at[0:256], 1),
+            (3, 256, arrived(group, 1, 1).at[256:512], 3),
         )[k]
         src = piece(group, 1, (place.y + offset) % 4, first, 256)
         return remote(src, dst, p1ys.at[group * 6 + k], p1yr.at[group * 6 + k], place.ys(to))
 
     def gradient(group, step):
-        tile = (place.y + jnp.where(step == 0, 2, jnp.where(step == 1, 1, jnp.where(step == 2, 3, 0)))) % 4
+        tile = tile_of(step)
         at = pl.ds(pl.multiple_of(tile * 512, 512), 512)
         lo = 0
         for axis, width in ((0, CX[group]), (1, CY[group])):
@@ -416,25 +508,42 @@
             out = tn(own_a[group][:, at], own[...]) + tn(other_a[group][:, at], oth[...])
             piece(group, axis, tile, 0, 512)[...] = out.astype(BF)
             lo += width
-        send_x(group, 0, tile).start()
-        send_x(group, 1, tile).start()
-        for k, when in ((0, 0), (2, 0), (1, 1), (3, 2)):
+        send_x(group, 0, step).start()
+
+        @pl.when(step == 0)
+        def _():
+            send_y(group, 0).start()
+            send_y(group, 2).start()
+
+    def near_x(group, step):
+        send_x(group, 1, step).start()
+
+    def near_y(group, step):
+        for when in (1, 2):
 
             @pl.when(step == when)
             def _():
-                send_y(group, k).start()
+                send_y(group, 2 * when - 1).start()
+
+    def all_near(group, *axes):
+        @pl.loop(0, 4)
+        def _(step):
+            for axis in axes:
+                (near_x, near_y)[axis](group, step)
 
     lands = ref["lands"]
 
     def mid_copies(group):
+        if group > 1:
+            return ()
         return (
-            pltpu.make_async_copy(relx[group], hid.at[:, 0 : CX[group]], lands.at[16 + group]),
-            pltpu.make_async_copy(rely[group], hid.at[:, 768 : 768 + CY[group]], lands.at[20 + group]),
+            pltpu.make_async_copy(relayed(group, 0), hid.at[:, 0 : CX[group]], lands.at[16 + group]),
+            pltpu.make_async_copy(relayed(group, 1), hid.at[:, 768 : 768 + CY[group]], lands.at[20 + group]),
         )
 
     def mid_start(group):
-        for tile in range(4):
-            send_x(group, 0, tile).wait_recv()
+        for step in range(4):
+            send_x(group, 0, step).wait_recv()
         for k in (0, 2):
             send_y(group, k).wait_recv()
         for copy in mid_copies(group):
@@ -445,16 +554,18 @@
             copy.wait()
 
         def add(axis, tile, first, rows, lo, width, count):
+            src = hid.at[:, lo : lo + width] if group < 2 else relayed(group, axis)
+
             @pl.loop(0, count // 32)
             def _(i):
                 own = piece(group, axis, tile, pl.multiple_of(first + i * 32, 32), 32)
-                got = hid[pl.ds(pl.multiple_of(rows + i * 32, 32), 32), lo : lo + width]
+                got = src[pl.ds(pl.multiple_of(rows + i * 32, 32), 32), :]
                 own[...] = (own[...].astype(F32) + got.astype(F32)).astype(BF)
 
-        for tile in range(4):
-            to = 1 if tile < 2 else 3
+        for step in range(4):
+            to, tile = (1, 3)[step % 2], tile_of(step)
             add(0, tile, ((place.x + to) % 4) * 128, tile * 128, 0, CX[group], 128)
-            send_x(group, 2, tile).start()
+            send_x(group, 2, step).start()
         for k, offset, first in ((4, 1, 0), (5, 3, 256)):
             add(1, (place.y + offset) % 4, first, first, 768, CY[group], 256)
             send_y(group, k).start()
@@ -470,13 +581,16 @@
             ggu[rows, n0:n1] = (up * sig * (1.0 + gate * (1.0 - sig))).astype(BF)
             ggu[rows, FF + n0 : FF + n1] = silu.astype(BF)
 
-    def feed_back(first, count, *sends):
+    def feed_back(first, count):
         rows = slice(first, first + count)
         for n0, n1 in ((0, 512), (512, 1024), (1024, 1408)):
             grad = nt(masked[rows, :], wd[n0:n1, :])
             for lo in (0, FF):
                 ggu[rows, lo + n0 : lo + n1] = (grad * ggu[rows, lo + n0 : lo + n1].astype(F32)).astype(BF)
 
+    def feed_part(first, count, *sends):
+        rows = slice(first, first + count)
+
         @pl.loop(0, 4)
         def _(n):
             at = pl.ds(pl.multiple_of(n * 512, 512), 512)
@@ -485,12 +599,14 @@
 
     feed(0, 128)
     feed_back(0, 128)
+    feed_part(0, 128)
     ag2.relay()
     agm.near()
     agm.relay()
     swap_masked(0).start()
     feed(128, 128)
-    feed_back(128, 128, 1, 3)
+    feed_back(128, 128)
+    feed_part(128, 128, 1, 3)
     swap_b(0).start()
     swap_b(2).start()
     ag2.near()
@@ -500,20 +616,42 @@
     swap_b(1).start()
     agm.far()
     swap_masked(1).start()
-    feed_back(256, 256, 0, 2)
+    feed_back(256, 256)
     swap_b(3).start()
     fetch(1)
+    feed_part(256, 256, 0, 2)
+    swap_b(0).wait_recv()
+    swap_b(1).wait_recv()
+    swap_masked(0).wait_recv()
+    swap_masked(1).wait_recv()
+
+    @pl.loop(0, 4)
+    def _(step):
+        gradient(0, step)
+        near_x(0, step)
+        near_y(0, step)
+
+        @pl.when(step < 3)
+        def _():
+            rs3.relay(jnp.where(step == 2, 3, step), jnp.where(step == 0, 1, jnp.where(step == 1, 3, 4)))
+    bring(1).wait()
+    swap_b(2).wait_recv()
+    swap_b(3).wait_recv()
+
+    @pl.loop(0, 2)
+    def _(step):
+        gradient(1, step)
 
     p2xs, p2xr, p2ys, p2yr = ref["p2xs"], ref["p2xr"], ref["p2ys"], ref["p2yr"]
 
     def landing(group):
         copies = []
-        for d in range(2):
-            for axis, src in ((0, recx[group]), (1, recy[group])):
+        for d in range(2 if group < 2 else 0):
+            for axis in range(2):
                 lo = d * FF + axis * 768
                 width = CX[group] if axis == 0 else CY[group]
                 sem = lands.at[group * 4 + d * 2 + axis]
-                copies.append(pltpu.make_async_copy(src.at[d], ggu.at[:, lo : lo + width], sem))
+                copies.append(pltpu.make_async_copy(arrived(group, axis, d), ggu.at[:, lo : lo + width], sem))
         return copies
 
     def send_2(group, axis, d):
@@ -528,9 +666,9 @@
         return remote(src, dst, p2ys.at[sem], p2yr.at[sem], place.xs(d))
 
     def land(group):
-        for tile in range(4):
+        for step in range(4):
             for kind in (1, 2):
-                send_x(group, kind, tile).wait_recv()
+                send_x(group, kind, step).wait_recv()
         for k in (1, 3, 4, 5):
             send_y(group, k).wait_recv()
         for copy in landing(group):
@@ -542,6 +680,10 @@
         for axis in range(2):
             lo = axis * 768
             width = CX[group] if axis == 0 else CY[group]
+            if group < 2:
+                got = [ggu.at[:, d * FF + lo : d * FF + lo + width] for d in range(2)]
+            else:
+                got = [arrived(group, axis, d) for d in range(2)]
 
             @pl.loop(0, 16)
             def _(i):
@@ -552,7 +694,7 @@
                 rows = pl.ds(pl.multiple_of(i * 32, 32), 32)
                 total = own[...].astype(F32)
                 for d in range(2):
-                    total = total + ggu[rows, d * FF + lo : d * FF + lo + width].astype(F32)
+                    total = total + got[d][rows, :].astype(F32)
                 own[...] = total.astype(BF)
 
             for d in (2, 1, 3):
@@ -591,30 +733,6 @@
                 whole[rows, first : first + width] = total
         for copy in ending(group):
             copy.start()
-
-    swap_b(0).wait_recv()
-    swap_b(1).wait_recv()
-    swap_masked(0).wait_recv()
-    swap_masked(1).wait_recv()
-
-    @pl.loop(0, 2)
-    def _(step):
-        gradient(0, step)
-
-    rs3.relay(0, 2)
-
-    @pl.loop(2, 4)
-    def _(step):
-        gradient(0, step)
-
-    rs3.relay(2, 4)
-    bring(1).wait()
-    swap_b(2).wait_recv()
-    swap_b(3).wait_recv()
-
-    @pl.loop(0, 2)
-    def _(step):
-        gradient(1, step)
 
     rs3.finish()
 
@@ -639,12 +757,14 @@
     gain2_part = lax.fori_loop(0, 8, mlp_back, jnp.zeros((1, D), F32))
     gacc[0, 4:8, :] = fold(gain2_part)
     ag4.start()
+    swap_branch(0).start()
     rs3.done()
 
     @pl.loop(2, 4)
     def _(step):
         gradient(1, step)
 
+    all_near(1, 0)
     @pl.loop(0, 4)
     def _(n):
         at = pl.ds(pl.multiple_of(n * 512, 512), 512)
@@ -656,16 +776,24 @@
     mid_start(0)
     ag4.relay()
 
-    @pl.loop(0, 4)
-    def _(n):
-        rs2.start(n, 0, 2, 1, 3)
-
     mid_end(0)
     mid_start(1)
     mid_end(1)
+    all_near(1, 1)
     ag4.near()
+    swap_branch(1).start()
+    swap_branch(2).start()
     ag4.far()
-    swap_a(2).start()
+    swap_branch(3).start()
+
+    @pl.loop(0, 4)
+    def _(n):
+        rs2.start(n, 0, 2)
+
+    @pl.loop(0, 4)
+    def _(n):
+        rs2.start(n, 1, 3)
+
 
     @pl.loop(0, 2)
     def _(n):
@@ -676,8 +804,7 @@
     def turn_back(v, rows):
         return v * cos_t[rows, :] - pltpu.roll(v, 64, 1) * sin_t[rows, :]
 
-    @pl.loop(0, HEADS)
-    def _(h):
+    def heads_back(h):
         def cols(j):
             return pl.ds(pl.multiple_of(j * 512 + h * HD, HD), HD)
 
@@ -700,36 +827,17 @@
             gproj[lo, cols(j)] = low
             gproj[hi, cols(j)] = high
 
+    pl.loop(0, HEADS // 2)(heads_back)
     fetch(2)
+    pl.loop(HEADS // 2, HEADS)(heads_back)
     swap_b(5).start()
-
-    def attn_part(n):
+    @pl.loop(0, 4)
+    def _(n):
         at = pl.ds(pl.multiple_of(n * 512, 512), 512)
         part = nt(in_order(place, gproj, slice(None)), wq[at, :])
         rs4.part[:, at] = part.astype(BF)
-        rs4.start(n, 0, 2, 1, 3)
         seen = jnp.sum(part * in_order(place, attn, at).astype(F32), axis=0, keepdims=True)
         gsum[n] = jnp.broadcast_to(seen, (8, 512))
-
-    @pl.loop(0, 2)
-    def _(n):
-        attn_part(n)
-
-    rs2.relay(0, 4)
-    land(0)
-    first_sum(0)
-    swap_a(1).wait_send()
-    ag2.done()
-    bring(3).wait()
-    swap_b(5).wait_recv()
-
-    @pl.loop(0, 4)
-    def _(step):
-        gradient(3, step)
-
-    @pl.loop(2, 4)
-    def _(n):
-        attn_part(n)
 
     for n in range(4):
         at = slice(n * 512, (n + 1) * 512)
@@ -762,6 +870,30 @@
         gacc[stage + 1] = total
 
     spread_start(0)
+
+    @pl.loop(0, 4)
+    def _(n):
+        rs4.start(n, 0, 2)
+
+    @pl.loop(0, 4)
+    def _(n):
+        rs4.start(n, 1, 3)
+
+    land(0)
+    first_sum(0)
+    swap_a(1).wait_send()
+    ag2.done()
+    bring(3).wait()
+    swap_b(5).wait_recv()
+
+    @pl.loop(0, 4)
+    def _(step):
+        gradient(3, step)
+
+    all_near(3, 0, 1)
+    rs2.relay(0, 4)
+    spread_end(0)
+    spread_start(1)
     swap_b(4).wait_recv()
     bring(2).wait()
 
@@ -769,9 +901,18 @@
     def _(step):
         gradient(2, step)
 
+    all_near(2, 0, 1)
+    mid_start(3)
+    mid_end(3)
+    spread_end(1)
+    spread_start(2)
+    rs4.relay(0, 4)
+    mid_start(2)
+    mid_end(2)
     land(1)
     first_sum(1)
-    rs4.relay(0, 4)
+    spread_end(2)
+    spread_start(3)
     rs2.finish()
 
     @pl.loop(0, 8)
@@ -781,23 +922,11 @@
 
     out_copy = pltpu.make_async_copy(middle, ref["output"], lsem.at[7])
     out_copy.start()
-    mid_start(3)
-    spread_end(0)
-    spread_start(1)
-    mid_end(3)
-    mid_start(2)
-    second_sum(0)
-    mid_end(2)
-    spread_end(1)
-    spread_start(2)
     land(3)
     first_sum(3)
     land(2)
     first_sum(2)
-    out_copy.wait()
-    second_sum(1)
-    spread_end(2)
-    spread_start(3)
+    second_sum(0)
     rs4.finish()
 
     @pl.loop(0, 8)
@@ -815,25 +944,28 @@
 
     tok_copy = pltpu.make_async_copy(gmid, ref["grad_tokens"], lsem.at[8])
     tok_copy.start()
+    spread_end(3)
+    ref["gains"][...] = gacc[4]
+    out_copy.wait()
+    second_sum(1)
     second_sum(3)
     second_sum(2)
-    spread_end(3)
-    ref["gains"][...] = gacc[4]
 
     for gather in (ag1, agm, ag4):
         gather.done()
     rs4.done()
     rs2.done()
-    for group in (2, 3):
-        swap_a(group).wait_send()
+    swap_a(3).wait_send()
+    for slot in range(4):
+        swap_branch(slot).wait_send()
     swap_masked(0).wait_send()
     swap_masked(1).wait_send()
     for k in (4, 5):
         swap_b(k).wait_send()
     for group in range(4):
-        for tile in range(4):
+        for step in range(4):
             for kind in range(3):
-                send_x(group, kind, tile).wait_send()
+                send_x(group, kind, step).wait_send()
         for k in range(6):
             send_y(group, k).wait_send()
         for d in (1, 2, 3):
@@ -863,8 +995,8 @@
         ("wd_h", w_down, hbm),
         ("cot", cotangent, hbm),
         ("lengths", lengths, smem),
-        ("cos", jnp.asarray(cos_t), vmem),
-        ("sin", jnp.asarray(sin_t), vmem),
+        ("cos_h", jnp.asarray(cos_t), hbm),
+        ("sin_h", jnp.asarray(sin_t), hbm),
     ]
     outs = [
         ("output", (ROWS, D), F32, hbm),
@@ -873,10 +1005,10 @@
         ("shares", (2, 64, ALL), F32, hbm),
         ("xa", (4, SEQ, D), BF, hbm),
     ]
-    outs += [(f"relx{g}", (SEQ, CX[g]), BF, hbm) for g in range(4)]
-    outs += [(f"rely{g}", (SEQ, CY[g]), BF, hbm) for g in range(4)]
-    outs += [(f"recx{g}", (2, SEQ, CX[g]), BF, hbm) for g in range(4)]
-    outs += [(f"recy{g}", (2, SEQ, CY[g]), BF, hbm) for g in range(4)]
+    outs += [(f"relx{g}", (SEQ, CX[g]), BF, hbm) for g in range(2)]
+    outs += [(f"rely{g}", (SEQ, CY[g]), BF, hbm) for g in range(2)]
+    outs += [(f"recx{g}", (2, SEQ, CX[g]), BF, hbm) for g in range(2)]
+    outs += [(f"recy{g}", (2, SEQ, CY[g]), BF, hbm) for g in range(2)]
     dma = pltpu.SemaphoreType.DMA
     scratch = [
         ("wq", pltpu.VMEM((D, 1536), BF)),
@@ -890,7 +1022,6 @@
         ("middle", pltpu.VMEM((ROWS, D), F32)),
         ("mlp", pltpu.VMEM((SEQ, D), BF)),
         ("masked", pltpu.VMEM((SEQ, D), BF)),
-        ("branch", pltpu.VMEM((SEQ, D), BF)),
         ("hid", pltpu.VMEM((SEQ, FF), BF)),
         ("ggu", pltpu.VMEM((SEQ, 2 * FF), BF)),
         ("gctx", pltpu.VMEM((SEQ, 512), BF)),
@@ -899,23 +1030,24 @@
         ("xb1", pltpu.VMEM((SEQ, COLS[1]), BF)),
         ("xb2", pltpu.VMEM((SEQ, COLS[2]), BF)),
         ("gmid", pltpu.VMEM((ROWS, D), F32)),
-        ("pa", pltpu.VMEM((SEQ, D), BF)),
+        ("w3", pltpu.VMEM((3, SEQ, D), BF)),
         ("relay_a", pltpu.VMEM((2, 64, D), BF)),
         ("recv_a", pltpu.VMEM((2, ROWS, D), BF)),
-        ("pb", pltpu.VMEM((SEQ, D), BF)),
         ("relay_b", pltpu.VMEM((2, 64, D), BF)),
         ("recv_b", pltpu.VMEM((2, ROWS, D), BF)),
         ("r2", pltpu.VMEM((3, ROWS, ALL), BF)),
         ("final", pltpu.VMEM((ROWS, 1792), F32)),
         ("gacc", pltpu.VMEM((5, 8, 512), F32)),
+        ("cos", pltpu.VMEM((SEQ, HD), F32)),
+        ("sin", pltpu.VMEM((SEQ, HD), F32)),
         ("gsum", pltpu.VMEM((4, 8, 512), F32)),
         ("grecv", pltpu.VMEM((14, 8, 512), F32)),
         ("zs", dma((8, 24))),
         ("zr", dma((8, 24))),
         ("lsem", dma((13,))),
         ("osem", dma((4,))),
-        ("xs", dma((15,))),
-        ("xr", dma((15,))),
+        ("xs", dma((18,))),
+        ("xr", dma((18,))),
         ("p1xs", dma((48,))),
         ("p1xr", dma((48,))),
         ("p1ys", dma((24,))),
@@ -926,6 +1058,8 @@
         ("p2yr", dma((12,))),
         ("lands", dma((24,))),
         ("gs", dma((10,))),
+        ("ws", dma((26,))),
+        ("wr", dma((26,))),
         ("gr", dma((10,))),
     ]
     names = [i[0] for i in ins] + [o[0] for o in outs] + [s[0] for s in scratch]
@@ -946,41 +1080,57 @@
 def arrange_kernel(out_in, tok_in, gains, shares, output, grad_tokens, gain1, qkv, out, gain2, gate_up, down, *scratch):
     out_v, tok_v, shares_v, sem = scratch
     down_at, gu_at, out_at, qkv_at = BASE
-    loads = [
-        pltpu.make_async_copy(src, dst, sem.at[i])
-        for i, (src, dst) in enumerate(((out_in, out_v), (tok_in, tok_v), (shares, shares_v)))
-    ]
-    for load in loads:
-        load.start()
 
     def columns(core, first, count):
         return shares_v.at[core, :, first : first + count]
 
+    def through(src, buf, dst, half):
+        rows = slice(half * 64, half * 64 + 64)
+        return (src.at[rows], buf.at[rows]), ((buf.at[rows], dst.at[rows]),)
+
+    def of_shares(first, count, *stores):
+        cols = slice(first, first + count)
+        return (shares.at[:, :, cols], shares_v.at[:, :, cols]), stores
+
     moves = (
-        ((out_v, output),),
-        ((tok_v, grad_tokens),),
-        (
-            (columns(0, gu_at, FF), gate_up.at[0]),
-            (columns(1, gu_at, FF), gate_up.at[1]),
+        through(out_in, out_v, output, 0),
+        through(out_in, out_v, output, 1),
+        through(tok_in, tok_v, grad_tokens, 0),
+        through(tok_in, tok_v, grad_tokens, 1),
+        of_shares(gu_at, FF, (columns(0, gu_at, FF), gate_up.at[0]), (columns(1, gu_at, FF), gate_up.at[1])),
+        of_shares(
+            qkv_at,
+            768,
             (columns(0, qkv_at, 512), qkv.at[0]),
             (columns(0, qkv_at + 512, 256), qkv.at[1, :, 0:256]),
             (columns(1, qkv_at, 256), qkv.at[1, :, 256:512]),
             (columns(1, qkv_at + 256, 512), qkv.at[2]),
+        ),
+        of_shares(
+            down_at,
+            768,
             (columns(0, down_at, 768), down.at[:, 0:768]),
             (columns(1, down_at + 128, 640), down.at[:, 768:1408]),
+        ),
+        of_shares(
+            out_at,
+            256,
             (columns(0, out_at, 256), out.at[:, 0:256]),
             (columns(1, out_at, 256), out.at[:, 256:512]),
         ),
     )
+    loads = [pltpu.make_async_copy(*move[0], sem.at[i]) for i, move in enumerate(moves)]
+    for load in loads:
+        load.start()
     for i in range(4):
         at = slice(i * 512, (i + 1) * 512)
         gain1[:, at] = gains[i : i + 1, :]
         gain2[:, at] = gains[4 + i : 5 + i, :]
     stores = []
-    for load, group in zip(loads, moves):
+    for load, move in zip(loads, moves):
         load.wait()
-        for src, dst in group:
-            stores.append(pltpu.make_async_copy(src, dst, sem.at[3 + len(stores)]))
+        for src, dst in move[1]:
+            stores.append(pltpu.make_async_copy(src, dst, sem.at[len(moves) + len(stores)]))
             stores[-1].start()
     for store in stores:
         store.wait()
@@ -1008,7 +1158,7 @@
             pltpu.VMEM((ROWS, D), F32),
             pltpu.VMEM((ROWS, D), F32),
             pltpu.VMEM((2, 64, ALL), F32),
-            pltpu.SemaphoreType.DMA((15,)),
+            pltpu.SemaphoreType.DMA((22,)),
         ],
         compiler_params=pltpu.CompilerParams(vmem_limit_bytes=63 * 1024 * 1024),
         name="arrange",

time: 182 us -> 174 us (0.956)
  Pallas kernels: 181 us -> 171 us
    pallas_call x1, Pallas kernels: 176 us -> 167 us  [block(): pl.pallas_call(functools.partial(kernel, names), out_shape=[jax.ShapeDtyp...]
where the time goes in v3:
time: 174 us; the launch traced here: 172 us
  Pallas kernels  171 us (98%)
    pallas_call x1, Pallas kernels, block(): pl.pallas_call(functools.partial(kernel, names), out_shape=[jax.ShapeDtyp...  167 us
    pallas_call x1, Pallas kernels, arrange(): pl.pallas_call(arrange_kernel, out_shape=[jax.ShapeDtypeStruct(o[0], F32)...  4.39 us

profile of v3, /device:TPU:1, one launch (start us, length us, event | category | flops | bytes accessed | tf_op | source)
XLA Modules:
  0.0 172.5 jit_solution(16817637048113543008)
XLA Ops:
  1.3 166.6 %block.1 = (f32[128,2048]{1,0:T(8,128)}, f32[128,2048]{1,0:T(8,128)}, f32[8,512]{1,0:T(8,128)}, f32[2,64,3200]{2,1,0:T(8,128)}, bf16[4,512,2048]{2,1,0:T(8,128)(...) custom-call(bf16[128,2048]{1,0:T(8,128)(2,1)} %refs_0_.1, ...), custom_call_target="tpu_custom_call" | custom-call | tf_op jit(solution)/shard_map/block/pallas_call | solution.py:1066
  167.9 4.4 %arrange.1 = (f32[128,2048]{1,0:T(8,128)}, f32[128,2048]{1,0:T(8,128)}, f32[1,2048]{1,0:T(1,128)}, f32[3,64,512]{2,1,0:T(8,128)}, f32[64,512]{1,0:T(8,128)}, /*i...) custom-call(f32[128,2048]{1,0:T(8,128)} %get-tuple-element.20.out_in, ...), custom_call_target="tpu_custom_call" | custom-call | tf_op jit(solution)/shard_map/arrange/pallas_call | solution.py:1152

commit v4 on v3

--- a/solution.py
+++ b/solution.py
@@ -274,7 +274,7 @@
         part = w3.at[:, w_rows(half, (major[half] + d) % 4, 64), halves[half]]
         return remote(part, part, ws.at[18 + half * 4 + d], wr.at[18 + half * 4 + d], place.core())
 
-    both = [(half, d) for half in range(2) for d in (1, 2, 3)]
+    both = [(half, d) for d in (1, 3, 2) for half in range(2)]
     for half, d in both:
         w_first(half, d).start()
     ag1.start()
@@ -321,9 +321,19 @@
     project(2)
     ag1.far()
     project(3)
-
-    @pl.loop(0, HEADS)
-    def _(h):
+    for half, d in both[:4]:
+        w_plane(half, 1, d).wait_recv()
+        w_core(half, 4 - d).start()
+
+    heads = ref["recv_a"].at[0]
+
+    def to_rows(d, pair):
+        src = ctx.at[pl.ds(pl.multiple_of(((place.t + d) % 4) * 128, 128), 128), pair * 256 : pair * 256 + 256]
+        dst = heads.at[:, pl.ds(pl.multiple_of(place.t * 512 + pair * 256, 256), 256)]
+        sem = pair * 3 + d - 1
+        return remote(src, dst, zs.at[4, sem], zr.at[4, sem], place.z(d))
+
+    def heads_forward(h):
         def cols(j):
             return pl.ds(pl.multiple_of(j * 512 + h * HD, HD), HD)
 
@@ -338,22 +348,17 @@
             probs[h, rows, 0:keys] = p
             ctx[rows, cols(0)] = nn(p, qkv[0:keys, cols(2)]).astype(BF)
 
-    heads = ref["recv_a"].at[0]
-
-    def to_rows(d):
-        src = ctx.at[pl.ds(pl.multiple_of(((place.t + d) % 4) * 128, 128), 128)]
-        dst = heads.at[:, pl.ds(pl.multiple_of(place.t * 512, 512), 512)]
-        return remote(src, dst, zs.at[4, d - 1], zr.at[4, d - 1], place.z(d))
-
-    for d in (1, 3, 2):
-        to_rows(d).start()
-    agm.start(1, 3)
+    for pair in range(2):
+        pl.loop(2 * pair, 2 * pair + 2)(heads_forward)
+        for d in (2, 1, 3):
+            to_rows(d, pair).start()
     own = pl.ds(pl.multiple_of(place.t * 128, 128), 128)
     heads[:, pl.ds(pl.multiple_of(place.t * 512, 512), 512)] = ctx[own, :]
-    for half, d in both:
+    for half, d in both[4:]:
         w_plane(half, 1, d).wait_recv()
-        w_core(half, (4 - d) % 4).start()
+        w_core(half, 4 - d).start()
     loads[3].wait()
+    agm.start(1, 3)
 
     other = 1 - place.c
     xs, xr = ref["xs"], ref["xr"]
@@ -392,8 +397,11 @@
     for half in range(2):
         for d in range(4):
             w_core(half, d).wait_recv()
-    for d in (1, 2, 3):
-        to_rows(d).wait_recv()
+    w3_keep = pltpu.make_async_copy(w3, ref["w3_h"], lsem.at[8])
+    w3_keep.start()
+    for pair in range(2):
+        for d in (1, 2, 3):
+            to_rows(d, pair).wait_recv()
 
     @pl.loop(0, 4)
     def _(n):
@@ -412,8 +420,9 @@
         inv = lax.rsqrt(jnp.mean(v * v, axis=-1, keepdims=True) + EPS)
         mlp[rows, :] = (v * inv * gain2[...]).astype(BF)
 
-    for d in (1, 2, 3):
-        to_rows(d).wait_send()
+    for pair in range(2):
+        for d in (1, 2, 3):
+            to_rows(d, pair).wait_send()
     for half, d in both:
         w_first(half, d).wait_send()
         w_plane(half, 0, d).wait_send()
@@ -441,7 +450,7 @@
 
     def fetch(group):
         if group == 2:
-            for slot in range(4):
+            for slot in range(1, 4):
                 swap_branch(slot).wait_recv()
         else:
             swap_a(group).wait_recv()
@@ -599,7 +608,16 @@
 
     feed(0, 128)
     feed_back(0, 128)
+    w3_keep.wait()
     feed_part(0, 128)
+    w3_back = []
+    for j in range(3):
+        rows, cols = slice(j * 512, (j + 1) * 512), slice(j * 512, (j + 1) * 512)
+        kept = ref["w3_h"].at[j]
+        w3_back.append(pltpu.make_async_copy(kept.at[:, 0:1536], wq.at[rows], osem.at[4 + j]))
+        w3_back.append(pltpu.make_async_copy(kept.at[:, 1536:2048], wq.at[1536:2048, cols], osem.at[7 + j]))
+    for copy in w3_back:
+        copy.start()
     ag2.relay()
     agm.near()
     agm.relay()
@@ -619,29 +637,50 @@
     feed_back(256, 256)
     swap_b(3).start()
     fetch(1)
-    feed_part(256, 256, 0, 2)
+    late, taken = slice(256, 512), slice(FF, FF + COLS[0])
+
+    @pl.loop(0, 4)
+    def _(n):
+        at = pl.ds(pl.multiple_of(n * 512, 512), 512)
+        rs3.part[late, at] = nt(ggu[late, taken], wgu[at, taken]).astype(BF)
+
     swap_b(0).wait_recv()
     swap_b(1).wait_recv()
     swap_masked(0).wait_recv()
     swap_masked(1).wait_recv()
 
-    @pl.loop(0, 4)
+    @pl.loop(0, 2)
     def _(step):
         gradient(0, step)
         near_x(0, step)
         near_y(0, step)
 
-        @pl.when(step < 3)
-        def _():
-            rs3.relay(jnp.where(step == 2, 3, step), jnp.where(step == 0, 1, jnp.where(step == 1, 3, 4)))
+    @pl.loop(0, 4)
+    def _(n):
+        at = pl.ds(pl.multiple_of(n * 512, 512), 512)
+        part = nt(ggu[late, 0:FF], wgu[at, 0:FF]) + nt(ggu[late, FF + COLS[0] :], wgu[at, FF + COLS[0] :])
+        rs3.part[late, at] = (part + rs3.part[late, at].astype(F32)).astype(BF)
+        rs3.start(n, 0, 2)
+
+    @pl.loop(2, 4)
+    def _(step):
+        gradient(0, step)
+        near_x(0, step)
+        near_y(0, step)
+
+    rs3.relay(0, 3)
     bring(1).wait()
     swap_b(2).wait_recv()
     swap_b(3).wait_recv()
 
-    @pl.loop(0, 2)
-    def _(step):
+    def gate_up(step):
         gradient(1, step)
-
+        near_x(1, step)
+        near_y(1, step)
+
+    gate_up(0)
+    rs3.relay(3, 4)
+    pl.loop(1, 3)(gate_up)
     p2xs, p2xr, p2ys, p2yr = ref["p2xs"], ref["p2xr"], ref["p2ys"], ref["p2yr"]
 
     def landing(group):
@@ -756,15 +795,31 @@
 
     gain2_part = lax.fori_loop(0, 8, mlp_back, jnp.zeros((1, D), F32))
     gacc[0, 4:8, :] = fold(gain2_part)
+    agm.done()
+    swap_masked(0).wait_send()
+    swap_masked(1).wait_send()
+    for copy in w3_back:
+        copy.wait()
+    own = pl.ds(pl.multiple_of(place.t * 128, 128), 128)
+
+    def to_heads(j):
+        src = masked.at[128:256, j * 512 : (j + 1) * 512]
+        return remote(src, gctx.at[own], zs.at[4, 6 + j], zr.at[4, 6 + j], place.z(3 - j))
+
+    for j in (1, 0, 2):
+        at = slice(j * 512, (j + 1) * 512)
+        part = nt(branch[own, 0:1536], wq[at, :]) + nt(branch[own, 1536:2048], wq[1536:2048, at])
+        masked[128:256, at] = part.astype(BF)
+        to_heads(j).start()
+    gctx[own, :] = nt(branch[own, :], wo[...]).astype(BF)
     ag4.start()
+    for load in loads[:3]:
+        load.start()
     swap_branch(0).start()
     rs3.done()
 
-    @pl.loop(2, 4)
-    def _(step):
-        gradient(1, step)
-
-    all_near(1, 0)
+    gate_up(3)
+
     @pl.loop(0, 4)
     def _(n):
         at = pl.ds(pl.multiple_of(n * 512, 512), 512)
@@ -774,32 +829,18 @@
     for k in (0, 1, 2, 3):
         swap_b(k).wait_send()
     mid_start(0)
-    ag4.relay()
-
     mid_end(0)
     mid_start(1)
     mid_end(1)
-    all_near(1, 1)
-    ag4.near()
-    swap_branch(1).start()
-    swap_branch(2).start()
-    ag4.far()
-    swap_branch(3).start()
-
-    @pl.loop(0, 4)
-    def _(n):
-        rs2.start(n, 0, 2)
-
-    @pl.loop(0, 4)
-    def _(n):
-        rs2.start(n, 1, 3)
-
-
-    @pl.loop(0, 2)
-    def _(n):
-        at = pl.ds(pl.multiple_of(n * 256, 256), 256)
-        gctx[:, at] = nt(branch[...], wo[at, :]).astype(BF)
-
+    ag4.relay()
+    for pair in ((0, 2), (1, 3)):
+
+        @pl.loop(0, 4)
+        def _(n):
+            rs2.start(n, *pair)
+
+    for j in range(3):
+        to_heads(j).wait_recv()
 
     def turn_back(v, rows):
         return v * cos_t[rows, :] - pltpu.roll(v, 64, 1) * sin_t[rows, :]
@@ -827,10 +868,27 @@
             gproj[lo, cols(j)] = low
             gproj[hi, cols(j)] = high
 
-    pl.loop(0, HEADS // 2)(heads_back)
-    fetch(2)
-    pl.loop(HEADS // 2, HEADS)(heads_back)
+    pl.loop(0, HEADS)(heads_back)
+    swap_branch(0).wait_recv()
     swap_b(5).start()
+    land(0)
+    for load in loads[:3]:
+        load.wait()
+    first_sum(0)
+    swap_a(1).wait_send()
+    ag2.done()
+    bring(3).wait()
+    swap_b(5).wait_recv()
+
+    @pl.loop(0, 4)
+    def _(step):
+        gradient(3, step)
+
+    all_near(3, 0, 1)
+    ag4.near()
+    ag4.far()
+    for slot in (1, 2, 3):
+        swap_branch(slot).start()
     @pl.loop(0, 4)
     def _(n):
         at = pl.ds(pl.multiple_of(n * 512, 512), 512)
@@ -870,30 +928,17 @@
         gacc[stage + 1] = total
 
     spread_start(0)
-
-    @pl.loop(0, 4)
-    def _(n):
-        rs4.start(n, 0, 2)
-
-    @pl.loop(0, 4)
-    def _(n):
-        rs4.start(n, 1, 3)
-
-    land(0)
-    first_sum(0)
-    swap_a(1).wait_send()
-    ag2.done()
-    bring(3).wait()
-    swap_b(5).wait_recv()
-
-    @pl.loop(0, 4)
-    def _(step):
-        gradient(3, step)
-
-    all_near(3, 0, 1)
     rs2.relay(0, 4)
-    spread_end(0)
-    spread_start(1)
+
+    for pair in ((0, 2), (1, 3)):
+
+        @pl.loop(0, 4)
+        def _(n):
+            rs4.start(n, *pair)
+
+    fetch(2)
+    mid_start(3)
+    mid_end(3)
     swap_b(4).wait_recv()
     bring(2).wait()
 
@@ -902,17 +947,17 @@
         gradient(2, step)
 
     all_near(2, 0, 1)
-    mid_start(3)
-    mid_end(3)
+    spread_end(0)
+    spread_start(1)
+    land(1)
+    first_sum(1)
+    mid_start(2)
+    mid_end(2)
     spread_end(1)
     spread_start(2)
+    land(3)
+    first_sum(3)
     rs4.relay(0, 4)
-    mid_start(2)
-    mid_end(2)
-    land(1)
-    first_sum(1)
-    spread_end(2)
-    spread_start(3)
     rs2.finish()
 
     @pl.loop(0, 8)
@@ -922,11 +967,13 @@
 
     out_copy = pltpu.make_async_copy(middle, ref["output"], lsem.at[7])
     out_copy.start()
-    land(3)
-    first_sum(3)
+    second_sum(0)
+    spread_end(2)
+    spread_start(3)
     land(2)
     first_sum(2)
-    second_sum(0)
+    out_copy.wait()
+    second_sum(1)
     rs4.finish()
 
     @pl.loop(0, 8)
@@ -946,20 +993,18 @@
     tok_copy.start()
     spread_end(3)
     ref["gains"][...] = gacc[4]
-    out_copy.wait()
-    second_sum(1)
     second_sum(3)
     second_sum(2)
 
-    for gather in (ag1, agm, ag4):
+    for j in range(3):
+        to_heads(j).wait_send()
+    for gather in (ag1, ag4):
         gather.done()
     rs4.done()
     rs2.done()
     swap_a(3).wait_send()
     for slot in range(4):
         swap_branch(slot).wait_send()
-    swap_masked(0).wait_send()
-    swap_masked(1).wait_send()
     for k in (4, 5):
         swap_b(k).wait_send()
     for group in range(4):
@@ -1004,6 +1049,7 @@
         ("gains", (8, 512), F32, vmem),
         ("shares", (2, 64, ALL), F32, hbm),
         ("xa", (4, SEQ, D), BF, hbm),
+        ("w3_h", (3, SEQ, D), BF, hbm),
     ]
     outs += [(f"relx{g}", (SEQ, CX[g]), BF, hbm) for g in range(2)]
     outs += [(f"rely{g}", (SEQ, CY[g]), BF, hbm) for g in range(2)]
@@ -1045,7 +1091,7 @@
         ("zs", dma((8, 24))),
         ("zr", dma((8, 24))),
         ("lsem", dma((13,))),
-        ("osem", dma((4,))),
+        ("osem", dma((10,))),
         ("xs", dma((18,))),
         ("xr", dma((18,))),
         ("p1xs", dma((48,))),

time: 174 us -> 168 us (0.966)
  Pallas kernels: 171 us -> 166 us
    pallas_call x1, Pallas kernels: 167 us -> 162 us  [block(): pl.pallas_call(functools.partial(kernel, names), out_shape=[jax.ShapeDtyp...]
where the time goes in v4:
time: 168 us
  Pallas kernels  166 us (99%)
    pallas_call x1, Pallas kernels, block(): pl.pallas_call(functools.partial(kernel, names), out_shape=[jax.ShapeDtyp...  162 us
    pallas_call x1, Pallas kernels, arrange(): pl.pallas_call(arrange_kernel, out_shape=[jax.ShapeDtypeStruct(o[0], F32)...  4.39 us

profile of v4, /device:TPU:1, one launch (start us, length us, event | category | flops | bytes accessed | tf_op | source)
XLA Modules:
  0.0 167.9 jit_solution(2074336805713260926)
XLA Ops:
  1.3 162.0 %block.1 = (f32[128,2048]{1,0:T(8,128)}, f32[128,2048]{1,0:T(8,128)}, f32[8,512]{1,0:T(8,128)}, f32[2,64,3200]{2,1,0:T(8,128)}, bf16[4,512,2048]{2,1,0:T(8,128)(...) custom-call(bf16[128,2048]{1,0:T(8,128)(2,1)} %refs_0_.1, ...), custom_call_target="tpu_custom_call" | custom-call | tf_op jit(solution)/shard_map/block/pallas_call | solution.py:1112
  163.3 4.4 %arrange.1 = (f32[128,2048]{1,0:T(8,128)}, f32[128,2048]{1,0:T(8,128)}, f32[1,2048]{1,0:T(1,128)}, f32[3,64,512]{2,1,0:T(8,128)}, f32[64,512]{1,0:T(8,128)}, /*i...) custom-call(f32[128,2048]{1,0:T(8,128)} %get-tuple-element.20.out_in, ...), custom_call_target="tpu_custom_call" | custom-call | tf_op jit(solution)/shard_map/arrange/pallas_call | solution.py:1198

commit v5 on v4

--- a/solution.py
+++ b/solution.py
@@ -704,6 +704,34 @@
         dst = r2.at[d - 1, :, BASE[group] + CX[group] : BASE[group] + COLS[group]]
         return remote(src, dst, p2ys.at[sem], p2yr.at[sem], place.xs(d))
 
+    q2s, q2r = ref["q2s"], ref["q2r"]
+
+    def send_3(group, axis, k):
+        lo = BASE[group] + (0 if axis == 0 else CX[group])
+        cols = slice(lo, lo + (CX[group] if axis == 0 else CY[group]))
+        offset, first, slot, to = ((2, 0, 2, 1), (1, 64, 0, 1), (2, 64, 2, 3), (3, 0, 1, 3), (1, 0, 0, 1), (3, 64, 1, 3))[k]
+        if axis == 0:
+            src = piece(group, 0, (place.y + offset) % 4, pl.multiple_of(place.x * 128 + first, 64), 64)
+        else:
+            src = piece(group, 1, place.y, pl.multiple_of(((place.x + offset) % 4) * 128 + first, 64), 64)
+        device = (place.ys, place.xs)[axis](to)
+        sem = (group * 2 + axis) * 6 + k
+        return remote(src, r2.at[slot, first : first + 64, cols], q2s.at[sem], q2r.at[sem], device)
+
+    def mid_second(group):
+        for axis in range(2):
+            lo = BASE[group] + (0 if axis == 0 else CX[group])
+            cols = slice(lo, lo + (CX[group] if axis == 0 else CY[group]))
+            for k, out, offset, first in ((0, 4, 1, 0), (2, 5, 3, 64)):
+                send_3(group, axis, k).wait_recv()
+                if axis == 0:
+                    own = piece(group, 0, (place.y + offset) % 4, pl.multiple_of(place.x * 128 + first, 64), 64)
+                else:
+                    own = piece(group, 1, place.y, pl.multiple_of(((place.x + offset) % 4) * 128 + first, 64), 64)
+                got = r2[2, first : first + 64, cols]
+                own[...] = (own[...].astype(F32) + got.astype(F32)).astype(BF)
+                send_3(group, axis, out).start()
+
     def land(group):
         for step in range(4):
             for kind in (1, 2):
@@ -736,8 +764,12 @@
                     total = total + got[d][rows, :].astype(F32)
                 own[...] = total.astype(BF)
 
-            for d in (2, 1, 3):
-                send_2(group, axis, d).start()
+            if group < 2:
+                for k in (0, 2, 1, 3):
+                    send_3(group, axis, k).start()
+            else:
+                for d in (2, 1, 3):
+                    send_2(group, axis, d).start()
 
     def whole_of(group):
         return ((final, 0), (middle, 0), (final, 768), (final, 1024))[group]
@@ -755,8 +787,12 @@
 
     def second_sum(group):
         for axis in range(2):
-            for d in (1, 2, 3):
-                send_2(group, axis, d).wait_recv()
+            if group < 2:
+                for k in (1, 3, 4, 5):
+                    send_3(group, axis, k).wait_recv()
+            else:
+                for d in (1, 2, 3):
+                    send_2(group, axis, d).wait_recv()
             lo = BASE[group] + (0 if axis == 0 else CX[group])
             width = CX[group] if axis == 0 else CY[group]
             whole, first = whole_of(group)
@@ -767,7 +803,7 @@
                 rows = pl.ds(pl.multiple_of(i * 32, 32), 32)
                 own = piece(group, axis, place.y, pl.multiple_of(place.x * 128 + i * 32, 32), 32)
                 total = own[...].astype(F32)
-                for d in range(3):
+                for d in range(2 if group < 2 else 3):
                     total = total + r2[d, rows, lo : lo + width].astype(F32)
                 whole[rows, first : first + width] = total
         for copy in ending(group):
@@ -928,14 +964,14 @@
         gacc[stage + 1] = total
 
     spread_start(0)
-    rs2.relay(0, 4)
-
     for pair in ((0, 2), (1, 3)):
 
         @pl.loop(0, 4)
         def _(n):
             rs4.start(n, *pair)
 
+    rs2.relay(0, 4)
+    mid_second(0)
     fetch(2)
     mid_start(3)
     mid_end(3)
@@ -953,11 +989,12 @@
     first_sum(1)
     mid_start(2)
     mid_end(2)
+    land(3)
+    first_sum(3)
+    mid_second(1)
+    rs4.relay(0, 4)
     spread_end(1)
     spread_start(2)
-    land(3)
-    first_sum(3)
-    rs4.relay(0, 4)
     rs2.finish()
 
     @pl.loop(0, 8)
@@ -968,12 +1005,12 @@
     out_copy = pltpu.make_async_copy(middle, ref["output"], lsem.at[7])
     out_copy.start()
     second_sum(0)
-    spread_end(2)
-    spread_start(3)
     land(2)
     first_sum(2)
     out_copy.wait()
     second_sum(1)
+    spread_end(2)
+    spread_start(3)
     rs4.finish()
 
     @pl.loop(0, 8)
@@ -1013,9 +1050,13 @@
                 send_x(group, kind, step).wait_send()
         for k in range(6):
             send_y(group, k).wait_send()
-        for d in (1, 2, 3):
-            for axis in range(2):
-                send_2(group, axis, d).wait_send()
+        for axis in range(2):
+            if group < 2:
+                for k in range(6):
+                    send_3(group, axis, k).wait_send()
+            else:
+                for d in (1, 2, 3):
+                    send_2(group, axis, d).wait_send()
     for stage in range(4):
         for copy in spread(stage)[0]:
             copy.wait_send()
@@ -1098,6 +1139,8 @@
         ("p1xr", dma((48,))),
         ("p1ys", dma((24,))),
         ("p1yr", dma((24,))),
+        ("q2s", dma((24,))),
+        ("q2r", dma((24,))),
         ("p2xs", dma((12,))),
         ("p2xr", dma((12,))),
         ("p2ys", dma((12,))),

time: 168 us -> 167 us (level)
  no operation moved by 1% of the time
where the time goes in v5:
time: 167 us
  Pallas kernels  165 us (99%)
    pallas_call x1, Pallas kernels, block(): pl.pallas_call(functools.partial(kernel, names), out_shape=[jax.ShapeDtyp...  161 us
    pallas_call x1, Pallas kernels, arrange(): pl.pallas_call(arrange_kernel, out_shape=[jax.ShapeDtypeStruct(o[0], F32)...  4.39 us

profile of v5, /device:TPU:1, one launch (start us, length us, event | category | flops | bytes accessed | tf_op | source)
XLA Modules:
  0.0 166.7 jit_solution(17159320309791232504)
XLA Ops:
  1.3 160.9 %block.1 = (f32[128,2048]{1,0:T(8,128)}, f32[128,2048]{1,0:T(8,128)}, f32[8,512]{1,0:T(8,128)}, f32[2,64,3200]{2,1,0:T(8,128)}, bf16[4,512,2048]{2,1,0:T(8,128)(...) custom-call(bf16[128,2048]{1,0:T(8,128)(2,1)} %refs_0_.1, ...), custom_call_target="tpu_custom_call" | custom-call | tf_op jit(solution)/shard_map/block/pallas_call | solution.py:1155
  162.2 4.4 %arrange.1 = (f32[128,2048]{1,0:T(8,128)}, f32[128,2048]{1,0:T(8,128)}, f32[1,2048]{1,0:T(1,128)}, f32[3,64,512]{2,1,0:T(8,128)}, f32[64,512]{1,0:T(8,128)}, /*i...) custom-call(f32[128,2048]{1,0:T(8,128)} %get-tuple-element.20.out_in, ...), custom_call_target="tpu_custom_call" | custom-call | tf_op jit(solution)/shard_map/arrange/pallas_call | solution.py:1241

commit v6 on v5

--- a/solution.py
+++ b/solution.py
@@ -1011,7 +1011,13 @@
     second_sum(1)
     spread_end(2)
     spread_start(3)
+    second_sum(3)
+    second_sum(2)
     rs4.finish()
+
+    def tok_copy(r):
+        rows = sixteen(r)
+        return pltpu.make_async_copy(gmid.at[rows], ref["grad_tokens"].at[rows], lsem.at[13 + r])
 
     @pl.loop(0, 8)
     def _(r):
@@ -1025,13 +1031,10 @@
             + inv * scaled
             - v * (inv * inv * inv) * jnp.mean(v * scaled, axis=-1, keepdims=True)
         )
-
-    tok_copy = pltpu.make_async_copy(gmid, ref["grad_tokens"], lsem.at[8])
-    tok_copy.start()
+        tok_copy(r).start()
+
     spread_end(3)
     ref["gains"][...] = gacc[4]
-    second_sum(3)
-    second_sum(2)
 
     for j in range(3):
         to_heads(j).wait_send()
@@ -1060,7 +1063,8 @@
     for stage in range(4):
         for copy in spread(stage)[0]:
             copy.wait_send()
-    tok_copy.wait()
+    for r in range(8):
+        tok_copy(r).wait()
     for group in range(4):
         for copy in ending(group):
             copy.wait()
@@ -1131,7 +1135,7 @@
         ("grecv", pltpu.VMEM((14, 8, 512), F32)),
         ("zs", dma((8, 24))),
         ("zr", dma((8, 24))),
-        ("lsem", dma((13,))),
+        ("lsem", dma((21,))),
         ("osem", dma((10,))),
         ("xs", dma((18,))),
         ("xr", dma((18,))),

time: 167 us -> 166 us (level)
  no operation moved by 1% of the time
where the time goes in v6:
time: 166 us
  Pallas kernels  165 us (99%)
    pallas_call x1, Pallas kernels, block(): pl.pallas_call(functools.partial(kernel, names), out_shape=[jax.ShapeDtyp...  160 us
    pallas_call x1, Pallas kernels, arrange(): pl.pallas_call(arrange_kernel, out_shape=[jax.ShapeDtypeStruct(o[0], F32)...  4.39 us

profile of v6, /device:TPU:1, one launch (start us, length us, event | category | flops | bytes accessed | tf_op | source)
XLA Modules:
  0.0 166.1 jit_solution(5720206984382594343)
XLA Ops:
  1.3 160.2 %block.1 = (f32[128,2048]{1,0:T(8,128)}, f32[128,2048]{1,0:T(8,128)}, f32[8,512]{1,0:T(8,128)}, f32[2,64,3200]{2,1,0:T(8,128)}, bf16[4,512,2048]{2,1,0:T(8,128)(...) custom-call(bf16[128,2048]{1,0:T(8,128)(2,1)} %refs_0_.1, ...), custom_call_target="tpu_custom_call" | custom-call | tf_op jit(solution)/shard_map/block/pallas_call | solution.py:1159
  161.5 4.4 %arrange.1 = (f32[128,2048]{1,0:T(8,128)}, f32[128,2048]{1,0:T(8,128)}, f32[1,2048]{1,0:T(1,128)}, f32[3,64,512]{2,1,0:T(8,128)}, f32[64,512]{1,0:T(8,128)}, /*i...) custom-call(f32[128,2048]{1,0:T(8,128)} %get-tuple-element.20.out_in, ...), custom_call_target="tpu_custom_call" | custom-call | tf_op jit(solution)/shard_map/arrange/pallas_call | solution.py:1245
